TPU v7x, 256 devices: a whole 4x4x8 slice. The times are simulated.
256 devices in a mesh: dp: 4 (over y), expert: 64 (over x, z, core).
Axes of the slice: x: 4, y: 4, z: 8, core: 2. Of those that a mesh axis runs over, the one named last changes fastest.
Arguments:
- tokens: bfloat16 [2048, 2048], P('dp'), may hold values from -6 to 6
- picks: int32 [2048, 8, 16], P('dp'), may hold values from 0 to 16383, all different within a row
- route_weight: float32 [2048, 8, 16], P('dp'), may hold values from 0.01 to 0.2
- out_grad: bfloat16 [2048, 2048], P('dp'), may hold values from -6 to 6
- down_rows: bfloat16 [16384, 2048], P('expert'), may hold values from -6 to 6
- up_rows: bfloat16 [16384, 2048], P('expert'), may hold values from -6 to 6
- down_mom: float32 [16384, 2048], P(('expert', 'dp')), may hold values from -1.5 to 1.5
- down_var: float32 [16384, 2048], P(('expert', 'dp')), may hold values from 0.0001 to 0.01
- up_mom: float32 [16384, 2048], P(('expert', 'dp')), may hold values from -1.5 to 1.5
- up_var: float32 [16384, 2048], P(('expert', 'dp')), may hold values from 0.0001 to 0.01
Outputs:
- layer_out: bfloat16 [2048, 2048], P('dp', 'expert')
- input_grad: bfloat16 [2048, 2048], P('dp', 'expert')
- new_down: bfloat16 [16384, 2048], P(('expert', 'dp'))
- new_up: bfloat16 [16384, 2048], P(('expert', 'dp'))
Inputs may be any that keep to these rules, and one draw needn't show every extreme that they name: `picks`: for each token and head the 16 picked experts are all different; the same expert may be picked by several heads of one token.
All inputs are finite; a program needn't handle non-finite values.
Results may differ from a plain program's by a relative error of at most 0.005.
Values may be sent and summed in bfloat16 or wider, within the bound.
A program may use at most 192 MiB of HBM per device.

v0:
```python
import math

import jax
import jax.numpy as jnp
from jax import lax
from jax.sharding import PartitionSpec as P

gelu_root = 0.7978845608
gelu_cube = 0.044715
learn_rate = 0.05
beta_one = 0.9
beta_two = 0.999
adam_eps = 1e-08


def gelu_value(inputs):
    inner = gelu_root * (inputs + gelu_cube * inputs * inputs * inputs)
    return 0.5 * inputs * (1.0 + jnp.tanh(inner))


def gelu_slope(inputs):
    tanh_part = jnp.tanh(gelu_root * (inputs + gelu_cube * inputs * inputs * inputs))
    return 0.5 * (1.0 + tanh_part) + 0.5 * inputs * (1.0 - tanh_part * tanh_part) * gelu_root * (
        1.0 + 3.0 * gelu_cube * inputs * inputs
    )


def adam_rows(rows, moment, second, grad):
    new_moment = beta_one * moment + (1.0 - beta_one) * grad
    new_second = beta_two * second + (1.0 - beta_two) * grad * grad
    updated = rows.astype(jnp.float32) - learn_rate * new_moment / (jnp.sqrt(new_second) + adam_eps)
    return updated.astype(jnp.bfloat16)


def local_coefficients(flat_ids, flat_weight, first_expert, local_count):
    blk_size = math.gcd(local_count, 64)
    n_blocks = local_count // blk_size

    def one_block(offset):
        block_ids = first_expert + offset + lax.iota(jnp.int32, blk_size)
        matched = flat_ids[None, :, :] == block_ids[:, None, None]
        return jnp.sum(
            jnp.where(matched, flat_weight[None, :, :], jnp.zeros_like(flat_weight[None, :, :])),
            axis=2,
        )

    offsets = lax.iota(jnp.int32, n_blocks) * blk_size
    return lax.map(one_block, offsets).reshape(local_count, flat_ids.shape[0])


def local(
    tokens, picks, route_weight, out_grad, down_rows, up_rows, down_mom, down_var, up_mom, up_var
):
    local_count = down_rows.shape[0]
    n_tok = tokens.shape[0]
    width_full = tokens.shape[1]
    inv_root = 1.0 / math.sqrt(width_full)
    flat_ids = picks.reshape(n_tok, -1)
    flat_weight = route_weight.reshape(n_tok, -1)
    owned = local_count // lax.axis_size("dp")
    first_expert = lax.axis_index("expert") * local_count
    coefficient = local_coefficients(flat_ids, flat_weight, first_expert, local_count)
    score = (
        jnp.einsum("ed,td->et", down_rows, tokens, preferred_element_type=jnp.float32) * inv_root
    )
    weighted = (coefficient * gelu_value(score)).astype(jnp.bfloat16)
    out_terms = jnp.einsum("et,ed->td", weighted, up_rows, preferred_element_type=jnp.float32)
    back = jnp.einsum("ed,td->et", up_rows, out_grad, preferred_element_type=jnp.float32)
    score_grad = (coefficient * gelu_slope(score) * back).astype(jnp.bfloat16)
    grad_terms = (
        jnp.einsum("et,ed->td", score_grad, down_rows, preferred_element_type=jnp.float32)
        * inv_root
    )
    joined = (
        lax.psum_scatter(out_terms, "expert", scatter_dimension=1, tiled=True),
        lax.psum_scatter(grad_terms, "expert", scatter_dimension=1, tiled=True),
    )
    layer_out = joined[0].astype(jnp.bfloat16)
    input_grad = joined[1].astype(jnp.bfloat16)
    down_part = (
        jnp.einsum("et,td->ed", score_grad, tokens, preferred_element_type=jnp.float32) * inv_root
    )
    up_part = jnp.einsum("et,td->ed", weighted, out_grad, preferred_element_type=jnp.float32)
    both_grads = lax.psum_scatter(
        jnp.concatenate([down_part, up_part], axis=1).astype(jnp.bfloat16),
        "dp",
        scatter_dimension=0,
        tiled=True,
    ).astype(jnp.float32)
    grad_down = both_grads[:, :width_full]
    grad_up = both_grads[:, width_full:]
    owner_start = lax.axis_index("dp") * owned
    own_down = lax.dynamic_slice_in_dim(down_rows, owner_start, owned, 0)
    own_up = lax.dynamic_slice_in_dim(up_rows, owner_start, owned, 0)
    new_down = adam_rows(own_down, down_mom, down_var, grad_down)
    new_up = adam_rows(own_up, up_mom, up_var, grad_up)
    return (layer_out, input_grad, new_down, new_up)


def solution(mesh):
    placed = (
        P("dp", None),
        P("dp", None, None),
        P("dp", None, None),
        P("dp", None),
        P("expert", None),
        P("expert", None),
        P(("expert", "dp"), None),
        P(("expert", "dp"), None),
        P(("expert", "dp"), None),
        P(("expert", "dp"), None),
    )
    return jax.shard_map(
        local,
        mesh=mesh,
        in_specs=placed,
        out_specs=(
            P("dp", "expert"),
            P("dp", "expert"),
            P(("expert", "dp"), None),
            P(("expert", "dp"), None),
        ),
        check_vma=False,
    )
```

profile of v0, /device:TPU:1, one launch (start us, length us, event | category | flops | bytes accessed | tf_op | source)
XLA Modules:
  0.0 380.6 jit_solution(9820106364333683615)
XLA Ops:
  7.2 32.0 %while.10 = (s32[]{:T(128)}, f32[4,64,512]{2,1,0:T(8,128)S(1)}, s32[512,8,16]{0,2,1:T(8,128)}, s32[4]{0:T(128)S(1)}, s32[]{:T(128)}, /*index=5*/f32[512,8,16]{0,2,1:T(8,128)}, s32[]{:T(128)}) while((s32[]{:T(128)}, f32[4,64,512]{2,1,0:T(8,128)S(1)}, s32[512,8,16]{0,2,1:T(8,128)}, s32[4]{0:T(128)S(1)}, s32[]{:T(128)}, ...), condition=%wide.region_2.3_spmd, body=%wide.region_0.2_spmd.sunk | while | flops 12550211 | bytes 1966709 | solution.py:48
  7.3 1.2 copy.22
  8.5 1.1 copy.23
  9.6 0.6 dynamic_slice.15
  10.8 4.5 %select_reduce_fusion.2 = f32[64,512]{1,0:T(8,128)S(1)} fusion(f32[512,128]{1,0:T(8,128)S(1)} %copy.22, s32[512,128]{1,0:T(8,128)S(1)} %copy.23, s32[64]{0:T(128)S(1)} %iota_add_fusion.2), kind=kLoop, calls=%fused_computation.clone.1 | loop fusion | flops 12550144 | bytes 655616 | tf_op jit(solution)/shard_map/while/body/eval_jaxpr/reduce_sum | solution.py:42
  15.4 1.1 copy.22
  16.4 1.1 copy.23
  17.5 0.6 dynamic_slice.15
  18.8 4.5 %select_reduce_fusion.2 = f32[64,512]{1,0:T(8,128)S(1)} fusion(f32[512,128]{1,0:T(8,128)S(1)} %copy.22, s32[512,128]{1,0:T(8,128)S(1)} %copy.23, s32[64]{0:T(128)S(1)} %iota_add_fusion.2), kind=kLoop, calls=%fused_computation.clone.1 | loop fusion | flops 12550144 | bytes 655616 | tf_op jit(solution)/shard_map/while/body/eval_jaxpr/reduce_sum | solution.py:42
  23.3 1.1 copy.22
  24.4 1.1 copy.23
  25.5 0.6 dynamic_slice.15
  26.8 4.5 %select_reduce_fusion.2 = f32[64,512]{1,0:T(8,128)S(1)} fusion(f32[512,128]{1,0:T(8,128)S(1)} %copy.22, s32[512,128]{1,0:T(8,128)S(1)} %copy.23, s32[64]{0:T(128)S(1)} %iota_add_fusion.2), kind=kLoop, calls=%fused_computation.clone.1 | loop fusion | flops 12550144 | bytes 655616 | tf_op jit(solution)/shard_map/while/body/eval_jaxpr/reduce_sum | solution.py:42
  31.3 1.1 copy.22
  32.4 1.1 copy.23
  34.7 4.5 %select_reduce_fusion.2 = f32[64,512]{1,0:T(8,128)S(1)} fusion(f32[512,128]{1,0:T(8,128)S(1)} %copy.22, s32[512,128]{1,0:T(8,128)S(1)} %copy.23, s32[64]{0:T(128)S(1)} %iota_add_fusion.2), kind=kLoop, calls=%fused_computation.clone.1 | loop fusion | flops 12550144 | bytes 655616 | tf_op jit(solution)/shard_map/while/body/eval_jaxpr/reduce_sum | solution.py:42
  39.3 2.4 bitcast_multiply_fusion
  41.8 0.7 convolution_convert_fusion
  43.0 0.9 fusion.1
  43.9 0.7 copy-done.3
  44.6 0.7 fusion
  45.3 1.6 pad_maximum_fusion
  47.0 2.7 fusion.18
  49.7 0.9 copy-done.4
  50.6 4.0 %convolution_multiply_fusion = f32[512,2048]{0,1:T(8,128)} fusion(bf16[256,512]{1,0:T(8,128)(2,1)S(1)} %copy-done.4, bf16[256,2048]{1,0:T(8,128)(2,1)} %param.16), kind=kOutput, calls=%fused_computation.3 | convolution fusion | flops 537919488 | bytes 5505024 | tf_op jit(solution)/shard_map/et,ed->td/dot_general | solution.py:71
  54.6 28.6 %reduce-scatter.8.cloned.1.call-done = bf16[64,4096]{1,0:T(8,128)(2,1)} async-done(((bf16[256,4096]{1,0:T(8,128)(2,1)}), bf16[64,4096]{1,0:T(8,128)(2,1)}) %reduce-scatter.8.cloned.1.call-update) | async-done | bytes 524304 | tf_op jit(solution)/shard_map/reduce_scatter | solution.py:84
  83.2 1.1 convert_element_type.33
  84.3 3.1 fusion.16
  87.4 138.9 %reduce-scatter.4.cloned.1.call-done = f32[512,32]{0,1:T(8,128)} async-done(((f32[512,2048]{0,1:T(8,128)}), f32[512,32]{0,1:T(8,128)}) %reduce-scatter.4.cloned.1.call-update) | async-done | bytes 65552 | tf_op jit(solution)/shard_map/reduce_scatter | solution.py:75
  226.3 1.5 convert_element_type.29
  227.8 144.8 %reduce-scatter.6.cloned.1.call-done = f32[512,32]{0,1:T(8,128)} async-done(((f32[512,2048]{0,1:T(8,128)}), f32[512,32]{0,1:T(8,128)}) %reduce-scatter.6.cloned.1.call-update) | async-done | bytes 65552 | tf_op jit(solution)/shard_map/reduce_scatter | solution.py:76
  372.6 1.5 convert_element_type.31
  (25 shorter events, 1.3 us)
Async XLA Ops:
  7.2 32.1 %copy-start = (bf16[512,2048]{1,0:T(8,128)(2,1)S(1)}, bf16[512,2048]{1,0:T(8,128)(2,1)}, u32[]{:S(2)}) copy-start(bf16[512,2048]{1,0:T(8,128)(2,1)} %param.12) | copy-start | bytes 6291460
  7.2 76.0 %reduce-scatter.8.cloned.1.call-start = ((), (), s32[]{:S(2)}) async-start(), calls=%async_computation.5 | async-start | bytes 2621440 | tf_op jit(solution)/shard_map/reduce_scatter | solution.py:84
  39.3 2.5 copy-start.1
  41.7 1.2 copy-start.2
  43.9 0.7 copy-start.3
  46.9 179.4 %reduce-scatter.4.cloned.1.call-start = ((), (), s32[]{:S(2)}) async-start(), calls=%async_computation.3 | async-start | bytes 4259840 | tf_op jit(solution)/shard_map/reduce_scatter | solution.py:75
  49.7 0.9 copy-start.4
  49.7 322.9 %reduce-scatter.6.cloned.1.call-start = ((), (), s32[]{:S(2)}) async-start(), calls=%async_computation.4 | async-start | bytes 4259840 | tf_op jit(solution)/shard_map/reduce_scatter | solution.py:76
Sparse Core Ops, SparseCore 0:
  47.0 36.1 reduce-scatter.7
  87.9 138.4 reduce-scatter.3
  230.5 142.1 reduce-scatter.5
where the time goes:
time: 386 us; the launch traced here: 381 us
  waiting for transfers between devices  312 us (81%)
  other arithmetic  26.8 us (7%)
  between operations  13.9 us (4%)
  local copies, waits for them, and re-layouts  13.2 us (3%)
  matrix products  11.5 us (3%)
    reduce_scatter x1, waiting for transfers between devices, local(): lax.psum_scatter(grad_terms, 'expert', scatter_dimension=1, tiled=True)  145 us
    reduce_scatter x1, waiting for transfers between devices, local(): lax.psum_scatter(out_terms, 'expert', scatter_dimension=1, tiled=True)  139 us
    reduce_scatter x1, waiting for transfers between devices, local(): lax.psum_scatter(jnp.concatenate([down_part, up_part], axis=1).astype(jnp...  28.6 us
    reduce_sum x4, other arithmetic, one_block(): jnp.sum(jnp.where(matched, flat_weight[None, :, :], jnp.zeros_like(flat_w...  18.1 us
  transfers between devices with their start and end apart: 3, of which 3 were waited for; matrix products, arithmetic and copies ran while one was open for 3% of the time, Pallas kernels for 0%

commit v1 on v0

v1 whole, which is shorter than its diff:
```python
import functools
import math

import jax
import jax.numpy as jnp
from jax import lax
from jax.experimental import pallas as pl
from jax.experimental.pallas import tpu as pltpu
from jax.sharding import PartitionSpec as P

gelu_root = 0.7978845608
gelu_cube = 0.044715
learn_rate = 0.05
beta_one = 0.9
beta_two = 0.999
adam_eps = 1e-08

D = 2048
E = 256
T = 512
NP = 128
OWN = 64
YN, XN, ZN = 4, 4, 8
Q = 4
R = 64 // Q
C = 4
CW = 2 * D // C
INV = 1.0 / math.sqrt(D)
MESH = pl.DeviceIdType.MESH
f32 = jnp.float32
bf16 = jnp.bfloat16


def coefficient_kernel(picks_ref, weight_ref, coef_ref, key_ref):
    first = lax.axis_index("expert") * E
    key = picks_ref[...] - first
    own = jnp.logical_and(key >= 0, key < E)
    key_ref[...] = jnp.where(own, key, -1)
    rounds = jnp.max(jnp.sum(own.astype(jnp.int32), axis=0, keepdims=True))
    coef_ref[...] = jnp.zeros((E, T), f32)

    def one_round(_, last):
        keys = key_ref[...]
        now = jnp.max(jnp.where(keys < last, keys, -1), axis=0, keepdims=True)
        total = jnp.sum(
            jnp.where(keys == now, weight_ref[...], 0.0), axis=0, keepdims=True
        )
        ids = lax.broadcasted_iota(jnp.int32, (E, T), 0)
        coef_ref[...] = jnp.where(ids == now, total, coef_ref[...])
        return now

    lax.fori_loop(0, rounds, one_round, jnp.full((1, T), E, jnp.int32))


def coefficients(picks, weights):
    vmem = pl.BlockSpec(memory_space=pltpu.VMEM)
    return pl.pallas_call(
        coefficient_kernel,
        out_shape=jax.ShapeDtypeStruct((E, T), f32),
        in_specs=[vmem, vmem],
        out_specs=vmem,
        scratch_shapes=[pltpu.VMEM((NP, T), jnp.int32)],
        compiler_params=pltpu.CompilerParams(vmem_limit_bytes=16 * 1024 * 1024),
    )(picks, weights)


def main_kernel(
    tok_hbm, cot_hbm, down_hbm, up_hbm, coef_hbm, dm_hbm, dv_hbm, um_hbm, uv_hbm,
    outs_ref, new_ref,
    acts, rows, prow, ws, pws, coef, state,
    gbuf, y1, y2, xbuf, x1, x2, zsum, zrecv, fin, fpeer,
    load_sem, pair_send, pair_recv,
    y_send, y_recv, x_send, x_recv, z_send, z_recv,
):
    y = lax.axis_index("dp")
    e = lax.axis_index("expert")
    c = lax.rem(e, 2)
    z = lax.rem(e // 2, ZN)
    x = e // (2 * ZN)

    def at(xx, zz, cc):
        return (y, (xx * ZN + zz) * 2 + cc)

    sibling = at(x, z, 1 - c)
    xp, xm = lax.rem(x + 1, XN), lax.rem(x + XN - 1, XN)
    x_right, x_left = at(xp, z, c), at(xm, z, c)
    yp, ym = lax.rem(y + 1, YN), lax.rem(y + YN - 1, YN)
    y_right, y_left = (yp, e), (ym, e)
    z_peers = [lax.rem(z + k, ZN) for k in range(1, ZN)]
    xo, yo = lax.rem(x + 2, XN), lax.rem(y + 2, YN)

    loads = []
    for i, (src, dst) in enumerate((
        (down_hbm, rows.at[0]), (up_hbm, rows.at[1]),
        (tok_hbm, acts.at[0]), (cot_hbm, acts.at[1]), (coef_hbm, coef),
        (dm_hbm, state.at[0]), (dv_hbm, state.at[1]),
        (um_hbm, state.at[2]), (uv_hbm, state.at[3]),
    )):
        copy = pltpu.make_async_copy(src, dst, load_sem.at[i])
        copy.start()
        loads.append(copy)

    barrier = pltpu.get_barrier_semaphore()
    greet = [sibling, x_right, x_left, y_right, y_left]
    greet += [at(x, p, c) for p in z_peers]
    for who in greet:
        pl.semaphore_signal(barrier, inc=1, device_id=who, device_id_type=MESH)
    pl.semaphore_wait(barrier, len(greet))

    def remote(src, dst, send, recv, who):
        return pltpu.make_async_remote_copy(
            src_ref=src, dst_ref=dst, send_sem=send, recv_sem=recv,
            device_id=who, device_id_type=MESH,
        )

    loads[0].wait()
    loads[1].wait()
    send_rows = remote(rows.at[c], prow, pair_send.at[0], pair_recv.at[0], sibling)
    send_rows.start()
    loads[2].wait()
    loads[3].wait()
    loads[4].wait()

    def score_step(i, carry):
        cols = pl.ds(pl.multiple_of(i * 128, 128), 128)
        s = lax.dot_general(
            rows[0], acts[0, cols, :], (((1,), (1,)), ((), ())),
            preferred_element_type=f32,
        ) * INV
        b = lax.dot_general(
            rows[1], acts[1, cols, :], (((1,), (1,)), ((), ())),
            preferred_element_type=f32,
        )
        k = coef[:, cols]
        u = jnp.tanh(gelu_root * (s + gelu_cube * s * s * s))
        ws[1, :, cols] = (k * (0.5 * s * (1.0 + u))).astype(bf16)
        slope = 0.5 * (1.0 + u) + 0.5 * s * (1.0 - u * u) * gelu_root * (
            1.0 + 3.0 * gelu_cube * s * s
        )
        ws[0, :, cols] = (k * slope * b).astype(bf16)
        return carry

    lax.fori_loop(0, T // 128, score_step, 0)
    send_ws = remote(ws.at[c], pws, pair_send.at[1], pair_recv.at[1], sibling)
    send_ws.start()

    def y_copy(q, kind, way):
        low = (kind != 1) == (way == 0)
        who, block = (y_right, yp) if way == 0 else (y_left, ym)
        if kind == 0:
            block = yo
        half = pl.ds(0 if low else OWN // 2, OWN // 2)
        src = gbuf.at[q, block, half, :]
        dst = y1.at[way, q] if kind == 0 else y2.at[way, q, half, :]
        return remote(src, dst, y_send.at[kind, way, q], y_recv.at[kind, way, q], who)

    for q in range(C):
        a, first = divmod(q * CW, D)

        def grad_step(i, carry, a=a, first=first, q=q):
            cols = pl.multiple_of(i * 256, 256)
            g = jnp.dot(
                ws[a], acts[a, :, pl.ds(first + cols, 256)], preferred_element_type=f32
            )
            gbuf[q, :, :, pl.ds(cols, 256)] = g.astype(bf16).reshape(YN, OWN, 256)
            return carry

        lax.fori_loop(0, CW // 256, grad_step, 0)
        for kind in (0, 1):
            for way in (0, 1):
                y_copy(q, kind, way).start()

    def x_copy(q, kind, way):
        low = (kind != 1) == (way == 0)
        who, block = (x_right, xp) if way == 0 else (x_left, xm)
        if kind == 0:
            block = xo
        half = pl.ds(0 if low else ZN // 2, ZN // 2)
        src = xbuf.at[block, q, half]
        dst = x1.at[way, q] if kind == 0 else x2.at[way, q, half]
        return remote(src, dst, x_send.at[kind, way, q], x_recv.at[kind, way, q], who)

    send_rows.wait_recv()
    send_ws.wait_recv()

    def block_of(b):
        def tile(i, carry):
            cols = pl.ds(pl.multiple_of(b * 512 + i * 256, 256), 256)
            part = lax.dot_general(
                rows[1 - c, :, cols], ws[1 - c], (((0,), (0,)), ((), ())),
                preferred_element_type=f32,
            ) + lax.dot_general(
                prow[:, cols], pws[...], (((0,), (0,)), ((), ())),
                preferred_element_type=f32,
            )
            part = part.astype(bf16)
            for k in range(4):
                for q in range(Q):
                    r = k * 64 + q * R
                    xbuf[b, q, i * 4 + k] = part[r : r + R, :]
            return carry

        lax.fori_loop(0, 2, tile, 0)

    block_of(xo)
    for q in range(Q):
        x_copy(q, 0, 0).start()
        x_copy(q, 0, 1).start()
    block_of(xp)
    for q in range(Q):
        x_copy(q, 1, 0).start()
    block_of(xm)
    for q in range(Q):
        x_copy(q, 1, 1).start()
    block_of(x)

    for q in range(max(C, Q)):
        for way in (0, 1):
            if q < Q:
                x_copy(q, 0, way).wait_recv()
                block = xp if way == 0 else xm
                half = pl.ds(0 if way == 0 else ZN // 2, ZN // 2)
                mine = xbuf[block, q, half].astype(f32)
                xbuf[block, q, half] = (mine + x1[way, q].astype(f32)).astype(bf16)
                x_copy(q, 2, way).start()
            if q < C:
                y_copy(q, 0, way).wait_recv()
                block = yp if way == 0 else ym
                half = pl.ds(0 if way == 0 else OWN // 2, OWN // 2)
                mine = gbuf[q, block, half, :].astype(f32)
                gbuf[q, block, half, :] = (mine + y1[way, q].astype(f32)).astype(bf16)
                y_copy(q, 2, way).start()

    def z_copy(q, k):
        p = z_peers[k]
        return remote(
            zsum.at[q, p], zrecv.at[q, k], z_send.at[q, k], z_recv.at[q, k], at(x, p, c)
        )

    for i in range(5, 9):
        loads[i].wait()
    for q in range(max(C, Q)):
        if q < Q:
            for way in (0, 1):
                x_copy(q, 1, way).wait_recv()
                x_copy(q, 2, way).wait_recv()
            total = (
                xbuf[x, q].astype(f32) + x2[0, q].astype(f32) + x2[1, q].astype(f32)
            )
            zsum[q] = total.astype(bf16)
            for k in range(ZN - 1):
                z_copy(q, k).start()
        if q < C:
            for way in (0, 1):
                y_copy(q, 1, way).wait_recv()
                y_copy(q, 2, way).wait_recv()
            a, first = divmod(q * CW, D)

            def adam_step(i, carry, a=a, first=first, q=q):
                r = pl.ds(pl.multiple_of(i * 16, 16), 16)
                cols = pl.ds(first, CW)
                grad = (
                    gbuf[q, y, r, :].astype(f32)
                    + y2[0, q, r, :].astype(f32)
                    + y2[1, q, r, :].astype(f32)
                )
                if a == 0:
                    grad = grad * INV
                m = beta_one * state[2 * a, r, cols] + (1.0 - beta_one) * grad
                v = beta_two * state[2 * a + 1, r, cols] + (1.0 - beta_two) * grad * grad
                old = rows[a, pl.ds(pl.multiple_of(y * OWN + i * 16, 16), 16), cols]
                new = old.astype(f32) - learn_rate * m / (jnp.sqrt(v) + adam_eps)
                new_ref[a, r, cols] = new.astype(bf16)
                return carry

            lax.fori_loop(0, OWN // 16, adam_step, 0)

    scale = jnp.where(c == 1, INV, 1.0).astype(f32)
    for q in range(Q):
        total = zsum[q, z].astype(f32)
        for k in range(ZN - 1):
            z_copy(q, k).wait_recv()
            total = total + zrecv[q, k].astype(f32)
        fin[q * R // 32, pl.ds(q * R % 32, R), :] = (total * scale).astype(bf16)
    send_fin = remote(fin.at[1 - c], fpeer, pair_send.at[2], pair_recv.at[2], sibling)
    send_fin.start()
    outs_ref[1 - c] = fin[c]
    send_fin.wait_recv()
    outs_ref[c] = fpeer[...]

    send_rows.wait_send()
    send_ws.wait_send()
    send_fin.wait_send()
    for kind in range(3):
        for way in (0, 1):
            for q in range(C):
                y_copy(q, kind, way).wait_send()
            for q in range(Q):
                x_copy(q, kind, way).wait_send()
    for q in range(Q):
        for k in range(ZN - 1):
            z_copy(q, k).wait_send()


def exchange(tokens, out_grad, down_rows, up_rows, coef, dm, dv, um, uv):
    hbm = pl.BlockSpec(memory_space=pl.ANY)
    vmem = pl.BlockSpec(memory_space=pltpu.VMEM)
    dma = pltpu.SemaphoreType.DMA
    return pl.pallas_call(
        main_kernel,
        out_shape=(
            jax.ShapeDtypeStruct((2, 32, T), bf16),
            jax.ShapeDtypeStruct((2, OWN, D), bf16),
        ),
        in_specs=[hbm] * 9,
        out_specs=(vmem, vmem),
        scratch_shapes=[
            pltpu.VMEM((2, T, D), bf16),
            pltpu.VMEM((2, E, D), bf16),
            pltpu.VMEM((E, D), bf16),
            pltpu.VMEM((2, E, T), bf16),
            pltpu.VMEM((E, T), bf16),
            pltpu.VMEM((E, T), f32),
            pltpu.VMEM((4, OWN, D), f32),
            pltpu.VMEM((C, YN, OWN, CW), bf16),
            pltpu.VMEM((2, C, OWN // 2, CW), bf16),
            pltpu.VMEM((2, C, OWN, CW), bf16),
            pltpu.VMEM((XN, Q, ZN, R, T), bf16),
            pltpu.VMEM((2, Q, ZN // 2, R, T), bf16),
            pltpu.VMEM((2, Q, ZN, R, T), bf16),
            pltpu.VMEM((Q, ZN, R, T), bf16),
            pltpu.VMEM((Q, ZN - 1, R, T), bf16),
            pltpu.VMEM((2, 32, T), bf16),
            pltpu.VMEM((32, T), bf16),
            dma((9,)),
            dma((3,)),
            dma((3,)),
            dma((3, 2, C)),
            dma((3, 2, C)),
            dma((3, 2, Q)),
            dma((3, 2, Q)),
            dma((Q, ZN - 1)),
            dma((Q, ZN - 1)),
        ],
        compiler_params=pltpu.CompilerParams(
            collective_id=0, has_side_effects=True, vmem_limit_bytes=48 * 1024 * 1024
        ),
    )(tokens, out_grad, down_rows, up_rows, coef, dm, dv, um, uv)


def local(
    tokens, picks, route_weight, out_grad, down_rows, up_rows, down_mom, down_var, up_mom, up_var
):
    picks_t = picks.transpose(1, 2, 0).reshape(NP, T)
    weight_t = route_weight.transpose(1, 2, 0).reshape(NP, T)
    coef = coefficients(picks_t, weight_t)
    outs, new = exchange(
        tokens, out_grad, down_rows, up_rows, coef, down_mom, down_var, up_mom, up_var
    )
    return (outs[1].T, outs[0].T, new[0], new[1])


def solution(mesh):
    placed = (
        P("dp", None),
        P("dp", None, None),
        P("dp", None, None),
        P("dp", None),
        P("expert", None),
        P("expert", None),
        P(("expert", "dp"), None),
        P(("expert", "dp"), None),
        P(("expert", "dp"), None),
        P(("expert", "dp"), None),
    )
    return jax.shard_map(
        local,
        mesh=mesh,
        in_specs=placed,
        out_specs=(
            P("dp", "expert"),
            P("dp", "expert"),
            P(("expert", "dp"), None),
            P(("expert", "dp"), None),
        ),
        check_vma=False,
    )
```

time: 386 us -> 61.1 us (0.16); the launches traced: 381 us -> 60.7 us
  waiting for transfers between devices: 312 us -> 0 us
  Pallas kernels: 0 us -> 50.1 us
  other arithmetic: 26.8 us -> 0 us
  between operations: 13.9 us -> 0.67 us
  matrix products: 11.5 us -> 0 us
    reduce_scatter x3 -> x0, waiting for transfers between devices: 312 us -> none  [the longest x1 145 us: local(): lax.psum_scatter(grad_terms, 'expert', scatter_dimension=1, tiled=True)]
    pallas_call x0 -> x2, Pallas kernels: none -> 50.1 us  [the longest x1 49.1 us: exchange(): pl.pallas_call(main_kernel, out_shape=(jax.ShapeDtypeStruct((2, 32, T), b...]
    reduce_sum x4 -> x0, other arithmetic: 18.1 us -> none  [one_block(): jnp.sum(jnp.where(matched, flat_weight[None, :, :], jnp.zeros_like(flat_w...]
    dot_general x6 -> x0, matrix products: 11.5 us -> none  [the longest x1 3.96 us: local(): jnp.einsum('et,ed->td', score_grad, down_rows, preferred_element_type=jnp...]
    convert_element_type x4 -> x0, other arithmetic: 7.11 us -> none  [the longest x1 3.08 us: adam_rows(): return updated.astype(jnp.bfloat16)]
    unnamed x10 -> x16, local copies, waits for them, and re-layouts: 2.04 us -> 8.5 us
    broadcast_in_dim x4 -> x0, local copies, waits for them, and re-layouts: 4.42 us -> none  [one_block(): jnp.where(matched, flat_weight[None, :, :], jnp.zeros_like(flat_weight[No...]
    eq x4 -> x0, local copies, waits for them, and re-layouts: 4.3 us -> none  [one_block(): matched = flat_ids[None, :, :] == block_ids[:, None, None]]
  transfers between devices with their start and end apart: 3 -> 0, of which waited for: 3 -> 0; matrix products, arithmetic and copies ran while one was open for 3% -> 0% of each run, Pallas kernels for 0% -> 0%
where the time goes in v1:
time: 61.1 us; the launch traced here: 60.7 us
  Pallas kernels  50.1 us (82%)
  local copies, waits for them, and re-layouts  9.97 us (16%)
  between operations  0.67 us (1%)
    pallas_call x1, Pallas kernels, exchange(): pl.pallas_call(main_kernel, out_shape=(jax.ShapeDtypeStruct((2, 32, T), b...  49.1 us
    unnamed x16, local copies, waits for them, and re-layouts  8.5 us

profile of v1, /device:TPU:1, one launch (start us, length us, event | category | flops | bytes accessed | tf_op | source)
XLA Modules:
  0.0 60.7 jit_solution(14311663987776612646)
XLA Ops:
  0.6 0.0 copy-start.6
  0.6 0.9 %copy-done.6 = s32[512,8,16]{0,2,1:T(8,128)S(1)} copy-done((s32[512,8,16]{0,2,1:T(8,128)S(1)}, s32[512,8,16]{0,2,1:T(8,128)}, u32[]{:S(2)}) %copy-start.6) | copy-done | bytes 262168
  1.6 0.0 copy-start.7
  1.6 0.9 %copy-done.7 = f32[512,8,16]{0,2,1:T(8,128)S(1)} copy-done((f32[512,8,16]{0,2,1:T(8,128)S(1)}, f32[512,8,16]{0,2,1:T(8,128)}, u32[]{:S(2)}) %copy-start.7) | copy-done | bytes 262168
  2.5 1.0 %shard_map.129.coef_hbm = f32[256,512]{1,0:T(8,128)S(1)} custom-call(s32[128,512]{1,0:T(8,128)S(1)} %bitcast.18, f32[128,512]{1,0:T(8,128)S(1)} %bitcast.19), custom_call_target="tpu_custom_call" | custom-call | tf_op jit(solution)/shard_map/pallas_call | solution.py:57
  3.5 0.0 copy-start
  3.5 1.2 %copy-done = bf16[256,2048]{1,0:T(8,128)(2,1)S(1)} copy-done((bf16[256,2048]{1,0:T(8,128)(2,1)S(1)}, bf16[256,2048]{1,0:T(8,128)(2,1)}, u32[]{:S(2)}) %copy-start) | copy-done | bytes 1048600
  4.8 0.0 copy-start.1
  4.8 1.2 %copy-done.1 = bf16[256,2048]{1,0:T(8,128)(2,1)S(1)} copy-done((bf16[256,2048]{1,0:T(8,128)(2,1)S(1)}, bf16[256,2048]{1,0:T(8,128)(2,1)}, u32[]{:S(2)}) %copy-start.1) | copy-done | bytes 1048600
  6.0 0.0 copy-start.2
  6.0 1.0 %copy-done.2 = f32[64,2048]{1,0:T(8,128)S(1)} copy-done((f32[64,2048]{1,0:T(8,128)S(1)}, f32[64,2048]{1,0:T(8,128)}, u32[]{:S(2)}) %copy-start.2) | copy-done | bytes 524312
  7.0 0.0 copy-start.3
  7.0 1.0 %copy-done.3 = f32[64,2048]{1,0:T(8,128)S(1)} copy-done((f32[64,2048]{1,0:T(8,128)S(1)}, f32[64,2048]{1,0:T(8,128)}, u32[]{:S(2)}) %copy-start.3) | copy-done | bytes 524312
  8.1 0.0 copy-start.4
  8.1 1.0 %copy-done.4 = f32[64,2048]{1,0:T(8,128)S(1)} copy-done((f32[64,2048]{1,0:T(8,128)S(1)}, f32[64,2048]{1,0:T(8,128)}, u32[]{:S(2)}) %copy-start.4) | copy-done | bytes 524312
  9.1 0.0 copy-start.5
  9.1 1.0 %copy-done.5 = f32[64,2048]{1,0:T(8,128)S(1)} copy-done((f32[64,2048]{1,0:T(8,128)S(1)}, f32[64,2048]{1,0:T(8,128)}, u32[]{:S(2)}) %copy-start.5) | copy-done | bytes 524312
  10.2 49.1 %shard_map.130 = (bf16[2,32,512]{2,1,0:T(8,128)(2,1)S(1)}, bf16[2,64,2048]{2,1,0:T(8,128)(2,1)S(1)}) custom-call(bf16[512,2048]{1,0:T(8,128)(2,1)} %tok_hbm.1, bf16[512,2048]{1,0:T(8,128)(2,1)} %cot_hbm.1, bf16[256,2048]{1,0:T(8,128)(2,1)S(1)} %copy-done, bf16[256,2048]{1,0:T(8,128)(2,1)S(1)} %copy-done.1, f32[256,512]{1,0:T(8,128)S(1)} %shard_map.129.coef_hbm, ...), custom_call_target="tpu_custom_call" | custom-call | tf_op jit(solution)/shard_map/pallas_call | solution.py:309
  59.3 0.6 %slice_bitcast_fusion.2 = (bf16[512,32]{0,1:T(8,128)(2,1)}, bf16[512,32]{0,1:T(8,128)(2,1)}) fusion(bf16[2,32,512]{2,1,0:T(8,128)(2,1)S(1)} %get-tuple-element.6), kind=kLoop, calls=%fused_computation.2 | loop fusion | bytes 131072 | tf_op jit(solution)/shard_map/transpose | solution.py:360
  59.9 0.8 %slice_bitcast_fusion = (bf16[64,2048]{1,0:T(8,128)(2,1)}, bf16[64,2048]{1,0:T(8,128)(2,1)}) fusion(bf16[2,64,2048]{2,1,0:T(8,128)(2,1)S(1)} %get-tuple-element.7), kind=kLoop, calls=%fused_computation | loop fusion | bytes 1048576 | tf_op jit(solution)/shard_map/squeeze | solution.py:360
Async XLA Ops:
  0.6 1.0 %copy-start.6 = (s32[512,8,16]{0,2,1:T(8,128)S(1)}, s32[512,8,16]{0,2,1:T(8,128)}, u32[]{:S(2)}) copy-start(s32[512,8,16]{0,2,1:T(8,128)} %param.11) | copy-start | bytes 786436
  1.6 0.9 %copy-start.7 = (f32[512,8,16]{0,2,1:T(8,128)S(1)}, f32[512,8,16]{0,2,1:T(8,128)}, u32[]{:S(2)}) copy-start(f32[512,8,16]{0,2,1:T(8,128)} %param.12) | copy-start | bytes 786436
  3.5 1.2 %copy-start = (bf16[256,2048]{1,0:T(8,128)(2,1)S(1)}, bf16[256,2048]{1,0:T(8,128)(2,1)}, u32[]{:S(2)}) copy-start(bf16[256,2048]{1,0:T(8,128)(2,1)} %down_hbm.1) | copy-start | bytes 3145732
  4.8 1.2 %copy-start.1 = (bf16[256,2048]{1,0:T(8,128)(2,1)S(1)}, bf16[256,2048]{1,0:T(8,128)(2,1)}, u32[]{:S(2)}) copy-start(bf16[256,2048]{1,0:T(8,128)(2,1)} %up_hbm.1) | copy-start | bytes 3145732
  6.0 1.0 %copy-start.2 = (f32[64,2048]{1,0:T(8,128)S(1)}, f32[64,2048]{1,0:T(8,128)}, u32[]{:S(2)}) copy-start(f32[64,2048]{1,0:T(8,128)} %dm_hbm.1) | copy-start | bytes 1572868
  7.0 1.0 %copy-start.3 = (f32[64,2048]{1,0:T(8,128)S(1)}, f32[64,2048]{1,0:T(8,128)}, u32[]{:S(2)}) copy-start(f32[64,2048]{1,0:T(8,128)} %dv_hbm.1) | copy-start | bytes 1572868
  8.1 1.0 %copy-start.4 = (f32[64,2048]{1,0:T(8,128)S(1)}, f32[64,2048]{1,0:T(8,128)}, u32[]{:S(2)}) copy-start(f32[64,2048]{1,0:T(8,128)} %um_hbm.1) | copy-start | bytes 1572868
  9.1 1.0 %copy-start.5 = (f32[64,2048]{1,0:T(8,128)S(1)}, f32[64,2048]{1,0:T(8,128)}, u32[]{:S(2)}) copy-start(f32[64,2048]{1,0:T(8,128)} %uv_hbm.1) | copy-start | bytes 1572868

commit v2 on v1

--- a/solution.py
+++ b/solution.py
@@ -31,13 +31,27 @@
 bf16 = jnp.bfloat16
 
 
-def coefficient_kernel(picks_ref, weight_ref, coef_ref, key_ref):
+def coefficient_kernel(
+    picks_hbm, weight_hbm, down_hbm, tok_hbm, up_hbm, cot_hbm,
+    coef_ref, rows_ref, acts_ref, key_ref, weight_ref, sem,
+):
+    loads = []
+    for i, (src, dst) in enumerate((
+        (picks_hbm, key_ref), (weight_hbm, weight_ref),
+        (down_hbm, rows_ref.at[0]), (tok_hbm, acts_ref.at[0]),
+        (up_hbm, rows_ref.at[1]), (cot_hbm, acts_ref.at[1]),
+    )):
+        copy = pltpu.make_async_copy(src, dst, sem.at[i])
+        copy.start()
+        loads.append(copy)
+    coef_ref[...] = jnp.zeros((E, T), f32)
+    loads[0].wait()
     first = lax.axis_index("expert") * E
-    key = picks_ref[...] - first
+    key = key_ref[...] - first
     own = jnp.logical_and(key >= 0, key < E)
     key_ref[...] = jnp.where(own, key, -1)
     rounds = jnp.max(jnp.sum(own.astype(jnp.int32), axis=0, keepdims=True))
-    coef_ref[...] = jnp.zeros((E, T), f32)
+    loads[1].wait()
 
     def one_round(_, last):
         keys = key_ref[...]
@@ -50,24 +64,35 @@
         return now
 
     lax.fori_loop(0, rounds, one_round, jnp.full((1, T), E, jnp.int32))
-
-
-def coefficients(picks, weights):
+    for copy in loads[2:]:
+        copy.wait()
+
+
+def coefficients(picks, weights, down_rows, tokens, up_rows, out_grad):
     vmem = pl.BlockSpec(memory_space=pltpu.VMEM)
+    hbm = pl.BlockSpec(memory_space=pltpu.HBM)
     return pl.pallas_call(
         coefficient_kernel,
-        out_shape=jax.ShapeDtypeStruct((E, T), f32),
-        in_specs=[vmem, vmem],
-        out_specs=vmem,
-        scratch_shapes=[pltpu.VMEM((NP, T), jnp.int32)],
-        compiler_params=pltpu.CompilerParams(vmem_limit_bytes=16 * 1024 * 1024),
-    )(picks, weights)
+        out_shape=(
+            pltpu.VMEM((E, T), f32),
+            pltpu.VMEM((2, E, D), bf16),
+            pltpu.VMEM((2, T, D), bf16),
+        ),
+        in_specs=[hbm] * 6,
+        out_specs=(vmem, vmem, vmem),
+        scratch_shapes=[
+            pltpu.VMEM((NP, T), jnp.int32),
+            pltpu.VMEM((NP, T), f32),
+            pltpu.SemaphoreType.DMA((6,)),
+        ],
+        compiler_params=pltpu.CompilerParams(vmem_limit_bytes=24 * 1024 * 1024),
+    )(picks, weights, down_rows, tokens, up_rows, out_grad)
 
 
 def main_kernel(
-    tok_hbm, cot_hbm, down_hbm, up_hbm, coef_hbm, dm_hbm, dv_hbm, um_hbm, uv_hbm,
-    outs_ref, new_ref,
-    acts, rows, prow, ws, pws, coef, state,
+    coef, rows, acts, dm_hbm, dv_hbm, um_hbm, uv_hbm,
+    layer_ref, input_ref, down_ref, up_ref,
+    prow, ws, pws, state,
     gbuf, y1, y2, xbuf, x1, x2, zsum, zrecv, fin, fpeer,
     load_sem, pair_send, pair_recv,
     y_send, y_recv, x_send, x_recv, z_send, z_recv,
@@ -91,8 +116,6 @@
 
     loads = []
     for i, (src, dst) in enumerate((
-        (down_hbm, rows.at[0]), (up_hbm, rows.at[1]),
-        (tok_hbm, acts.at[0]), (cot_hbm, acts.at[1]), (coef_hbm, coef),
         (dm_hbm, state.at[0]), (dv_hbm, state.at[1]),
         (um_hbm, state.at[2]), (uv_hbm, state.at[3]),
     )):
@@ -105,7 +128,6 @@
     greet += [at(x, p, c) for p in z_peers]
     for who in greet:
         pl.semaphore_signal(barrier, inc=1, device_id=who, device_id_type=MESH)
-    pl.semaphore_wait(barrier, len(greet))
 
     def remote(src, dst, send, recv, who):
         return pltpu.make_async_remote_copy(
@@ -113,34 +135,22 @@
             device_id=who, device_id_type=MESH,
         )
 
-    loads[0].wait()
-    loads[1].wait()
+    s = lax.dot_general(
+        rows[0], acts[0], (((1,), (1,)), ((), ())), preferred_element_type=f32
+    ) * INV
+    b = lax.dot_general(
+        rows[1], acts[1], (((1,), (1,)), ((), ())), preferred_element_type=f32
+    )
+    k = coef[...]
+    u = jnp.tanh(gelu_root * (s + gelu_cube * s * s * s))
+    ws[1] = (k * (0.5 * s * (1.0 + u))).astype(bf16)
+    slope = 0.5 * (1.0 + u) + 0.5 * s * (1.0 - u * u) * gelu_root * (
+        1.0 + 3.0 * gelu_cube * s * s
+    )
+    ws[0] = (k * slope * b).astype(bf16)
+    pl.semaphore_wait(barrier, len(greet))
     send_rows = remote(rows.at[c], prow, pair_send.at[0], pair_recv.at[0], sibling)
     send_rows.start()
-    loads[2].wait()
-    loads[3].wait()
-    loads[4].wait()
-
-    def score_step(i, carry):
-        cols = pl.ds(pl.multiple_of(i * 128, 128), 128)
-        s = lax.dot_general(
-            rows[0], acts[0, cols, :], (((1,), (1,)), ((), ())),
-            preferred_element_type=f32,
-        ) * INV
-        b = lax.dot_general(
-            rows[1], acts[1, cols, :], (((1,), (1,)), ((), ())),
-            preferred_element_type=f32,
-        )
-        k = coef[:, cols]
-        u = jnp.tanh(gelu_root * (s + gelu_cube * s * s * s))
-        ws[1, :, cols] = (k * (0.5 * s * (1.0 + u))).astype(bf16)
-        slope = 0.5 * (1.0 + u) + 0.5 * s * (1.0 - u * u) * gelu_root * (
-            1.0 + 3.0 * gelu_cube * s * s
-        )
-        ws[0, :, cols] = (k * slope * b).astype(bf16)
-        return carry
-
-    lax.fori_loop(0, T // 128, score_step, 0)
     send_ws = remote(ws.at[c], pws, pair_send.at[1], pair_recv.at[1], sibling)
     send_ws.start()
 
@@ -156,16 +166,8 @@
 
     for q in range(C):
         a, first = divmod(q * CW, D)
-
-        def grad_step(i, carry, a=a, first=first, q=q):
-            cols = pl.multiple_of(i * 256, 256)
-            g = jnp.dot(
-                ws[a], acts[a, :, pl.ds(first + cols, 256)], preferred_element_type=f32
-            )
-            gbuf[q, :, :, pl.ds(cols, 256)] = g.astype(bf16).reshape(YN, OWN, 256)
-            return carry
-
-        lax.fori_loop(0, CW // 256, grad_step, 0)
+        g = jnp.dot(ws[a], acts[a, :, first : first + CW], preferred_element_type=f32)
+        gbuf[q] = g.astype(bf16).reshape(YN, OWN, CW)
         for kind in (0, 1):
             for way in (0, 1):
                 y_copy(q, kind, way).start()
@@ -184,23 +186,19 @@
     send_ws.wait_recv()
 
     def block_of(b):
-        def tile(i, carry):
-            cols = pl.ds(pl.multiple_of(b * 512 + i * 256, 256), 256)
-            part = lax.dot_general(
-                rows[1 - c, :, cols], ws[1 - c], (((0,), (0,)), ((), ())),
-                preferred_element_type=f32,
-            ) + lax.dot_general(
-                prow[:, cols], pws[...], (((0,), (0,)), ((), ())),
-                preferred_element_type=f32,
-            )
-            part = part.astype(bf16)
-            for k in range(4):
-                for q in range(Q):
-                    r = k * 64 + q * R
-                    xbuf[b, q, i * 4 + k] = part[r : r + R, :]
-            return carry
-
-        lax.fori_loop(0, 2, tile, 0)
+        cols = pl.ds(pl.multiple_of(b * 512, 512), 512)
+        part = lax.dot_general(
+            rows[1 - c, :, cols], ws[1 - c], (((0,), (0,)), ((), ())),
+            preferred_element_type=f32,
+        ) + lax.dot_general(
+            prow[:, cols], pws[...], (((0,), (0,)), ((), ())),
+            preferred_element_type=f32,
+        )
+        part = part.astype(bf16)
+        for k in range(ZN):
+            for q in range(Q):
+                r = k * 64 + q * R
+                xbuf[b, q, k] = part[r : r + R, :]
 
     block_of(xo)
     for q in range(Q):
@@ -237,8 +235,8 @@
             zsum.at[q, p], zrecv.at[q, k], z_send.at[q, k], z_recv.at[q, k], at(x, p, c)
         )
 
-    for i in range(5, 9):
-        loads[i].wait()
+    for copy in loads:
+        copy.wait()
     for q in range(max(C, Q)):
         if q < Q:
             for way in (0, 1):
@@ -270,7 +268,7 @@
                 v = beta_two * state[2 * a + 1, r, cols] + (1.0 - beta_two) * grad * grad
                 old = rows[a, pl.ds(pl.multiple_of(y * OWN + i * 16, 16), 16), cols]
                 new = old.astype(f32) - learn_rate * m / (jnp.sqrt(v) + adam_eps)
-                new_ref[a, r, cols] = new.astype(bf16)
+                (down_ref if a == 0 else up_ref)[r, cols] = new.astype(bf16)
                 return carry
 
             lax.fori_loop(0, OWN // 16, adam_step, 0)
@@ -284,9 +282,11 @@
         fin[q * R // 32, pl.ds(q * R % 32, R), :] = (total * scale).astype(bf16)
     send_fin = remote(fin.at[1 - c], fpeer, pair_send.at[2], pair_recv.at[2], sibling)
     send_fin.start()
-    outs_ref[1 - c] = fin[c]
+    mine = fin[c]
     send_fin.wait_recv()
-    outs_ref[c] = fpeer[...]
+    peer = fpeer[...]
+    layer_ref[...] = jnp.where(c == 0, mine, peer)
+    input_ref[...] = jnp.where(c == 0, peer, mine)
 
     send_rows.wait_send()
     send_ws.wait_send()
@@ -302,25 +302,24 @@
             z_copy(q, k).wait_send()
 
 
-def exchange(tokens, out_grad, down_rows, up_rows, coef, dm, dv, um, uv):
-    hbm = pl.BlockSpec(memory_space=pl.ANY)
+def exchange(coef, rows, acts, dm, dv, um, uv):
+    hbm = pl.BlockSpec(memory_space=pltpu.HBM)
     vmem = pl.BlockSpec(memory_space=pltpu.VMEM)
     dma = pltpu.SemaphoreType.DMA
     return pl.pallas_call(
         main_kernel,
         out_shape=(
-            jax.ShapeDtypeStruct((2, 32, T), bf16),
-            jax.ShapeDtypeStruct((2, OWN, D), bf16),
+            jax.ShapeDtypeStruct((32, T), bf16),
+            jax.ShapeDtypeStruct((32, T), bf16),
+            jax.ShapeDtypeStruct((OWN, D), bf16),
+            jax.ShapeDtypeStruct((OWN, D), bf16),
         ),
-        in_specs=[hbm] * 9,
-        out_specs=(vmem, vmem),
+        in_specs=[vmem] * 3 + [hbm] * 4,
+        out_specs=(vmem,) * 4,
         scratch_shapes=[
-            pltpu.VMEM((2, T, D), bf16),
-            pltpu.VMEM((2, E, D), bf16),
             pltpu.VMEM((E, D), bf16),
             pltpu.VMEM((2, E, T), bf16),
             pltpu.VMEM((E, T), bf16),
-            pltpu.VMEM((E, T), f32),
             pltpu.VMEM((4, OWN, D), f32),
             pltpu.VMEM((C, YN, OWN, CW), bf16),
             pltpu.VMEM((2, C, OWN // 2, CW), bf16),
@@ -332,7 +331,7 @@
             pltpu.VMEM((Q, ZN - 1, R, T), bf16),
             pltpu.VMEM((2, 32, T), bf16),
             pltpu.VMEM((32, T), bf16),
-            dma((9,)),
+            dma((4,)),
             dma((3,)),
             dma((3,)),
             dma((3, 2, C)),
@@ -343,9 +342,9 @@
             dma((Q, ZN - 1)),
         ],
         compiler_params=pltpu.CompilerParams(
-            collective_id=0, has_side_effects=True, vmem_limit_bytes=48 * 1024 * 1024
+            collective_id=0, has_side_effects=True, vmem_limit_bytes=36 * 1024 * 1024
         ),
-    )(tokens, out_grad, down_rows, up_rows, coef, dm, dv, um, uv)
+    )(coef, rows, acts, dm, dv, um, uv)
 
 
 def local(
@@ -353,11 +352,14 @@
 ):
     picks_t = picks.transpose(1, 2, 0).reshape(NP, T)
     weight_t = route_weight.transpose(1, 2, 0).reshape(NP, T)
-    coef = coefficients(picks_t, weight_t)
-    outs, new = exchange(
-        tokens, out_grad, down_rows, up_rows, coef, down_mom, down_var, up_mom, up_var
-    )
-    return (outs[1].T, outs[0].T, new[0], new[1])
+    in_hbm = functools.partial(pltpu.with_memory_space_constraint, memory_space=pltpu.HBM)
+    coef, rows, acts = coefficients(
+        *map(in_hbm, (picks_t, weight_t, down_rows, tokens, up_rows, out_grad))
+    )
+    layer, grad, new_down, new_up = exchange(
+        coef, rows, acts, *map(in_hbm, (down_mom, down_var, up_mom, up_var))
+    )
+    return (layer.T, grad.T, new_down, new_up)
 
 
 def solution(mesh):

time: 61.1 us -> 51.8 us (0.85)
  local copies, waits for them, and re-layouts: 9.97 us -> 2.64 us
  Pallas kernels: 50.1 us -> 48.4 us
    unnamed x16 -> x4, local copies, waits for them, and re-layouts: 8.5 us -> 2.64 us
    pallas_call x2, Pallas kernels: 50.1 us -> 48.4 us  [the longest x1 45.3 us: exchange(): pl.pallas_call(main_kernel, out_shape=(jax.ShapeDtypeStruct((32, T), bf16...]
    squeeze x1 -> x0, local copies, waits for them, and re-layouts: 0.83 us -> none  [local(): return (outs[1].T, outs[0].T, new[0], new[1])]
    transpose x1 -> x0, local copies, waits for them, and re-layouts: 0.63 us -> none  [local(): return (outs[1].T, outs[0].T, new[0], new[1])]
where the time goes in v2:
time: 51.8 us; the launch traced here: 51.7 us
  Pallas kernels  48.4 us (93%)
  local copies, waits for them, and re-layouts  2.64 us (5%)
  between operations  0.65 us (1%)
    pallas_call x1, Pallas kernels, exchange(): pl.pallas_call(main_kernel, out_shape=(jax.ShapeDtypeStruct((32, T), bf16...  45.3 us
    pallas_call x1, Pallas kernels, coefficients(): pl.pallas_call(coefficient_kernel, out_shape=(pltpu.VMEM((E, T), f32), pl...  3.1 us
    unnamed x4, local copies, waits for them, and re-layouts  2.64 us

profile of v2, /device:TPU:1, one launch (start us, length us, event | category | flops | bytes accessed | tf_op | source)
XLA Modules:
  0.0 51.7 jit_solution(14550421500160991929)
XLA Ops:
  0.6 3.1 %shard_map.129 = (f32[256,512]{1,0:T(8,128)S(1)}, bf16[2,256,2048]{2,1,0:T(8,128)(2,1)S(1)}, bf16[2,512,2048]{2,1,0:T(8,128)(2,1)S(1)}) custom-call(s32[128,512]{1,0:T(8,128)} %bitcast.10, f32[128,512]{1,0:T(8,128)} %bitcast.11, bf16[256,2048]{1,0:T(8,128)(2,1)} %down_hbm.1, bf16[512,2048]{1,0:T(8,128)(2,1)} %tok_hbm.1, bf16[256,2048]{1,0:T(8,128)(2,1)} %up_hbm.1, ...), custom_call_target="tpu_custom_call" | custom-call | tf_op jit(solution)/shard_map/pallas_call | solution.py:74
  3.7 45.3 %shard_map.130 = (bf16[32,512]{1,0:T(8,128)(2,1)S(1)}, bf16[32,512]{1,0:T(8,128)(2,1)S(1)}, bf16[64,2048]{1,0:T(8,128)(2,1)S(1)}, bf16[64,2048]{1,0:T(8,128)(2,1)S(1)}) custom-call(f32[256,512]{1,0:T(8,128)S(1)} %get-tuple-element.11.coef, bf16[2,256,2048]{2,1,0:T(8,128)(2,1)S(1)} %get-tuple-element.12.rows, ...), custom_call_target="tpu_custom_call" | custom-call | tf_op jit(solution)/shard_map/pallas_call | solution.py:309
  49.1 0.6 %copy.18 = bf16[512,32]{0,1:T(8,128)(2,1)} copy(bf16[512,32]{0,1:T(8,128)(2,1)S(1)} %bitcast.9) | data formatting | bytes 65536
  49.7 0.6 %copy.19 = bf16[512,32]{0,1:T(8,128)(2,1)} copy(bf16[512,32]{0,1:T(8,128)(2,1)S(1)} %bitcast.8) | data formatting | bytes 65536
  50.3 0.7 %copy.20 = bf16[64,2048]{1,0:T(8,128)(2,1)} copy(bf16[64,2048]{1,0:T(8,128)(2,1)S(1)} %get-tuple-element.24) | data formatting | bytes 524288
  51.0 0.7 %copy.21 = bf16[64,2048]{1,0:T(8,128)(2,1)} copy(bf16[64,2048]{1,0:T(8,128)(2,1)S(1)} %get-tuple-element.25) | data formatting | bytes 524288

commit v3 on v2

v3 whole, which is shorter than its diff:
```python
import functools
import math

import jax
import jax.numpy as jnp
from jax import lax
from jax.experimental import pallas as pl
from jax.experimental.pallas import tpu as pltpu
from jax.sharding import PartitionSpec as P

gelu_root = 0.7978845608
gelu_cube = 0.044715
learn_rate = 0.05
beta_one = 0.9
beta_two = 0.999
adam_eps = 1e-08

D = 2048
E = 256
T = 512
NP = 128
OWN = 64
YN, XN, ZN = 4, 4, 8
Q = 2
R = 64 // Q
TA = 256
TB = T - TA
C = 4
CW = 2 * D // C
INV = 1.0 / math.sqrt(D)
MESH = pl.DeviceIdType.MESH
f32 = jnp.float32
bf16 = jnp.bfloat16


def coefficient_kernel(
    picks_hbm, weight_hbm, down_hbm, tok_hbm, up_hbm, cot_hbm,
    coef_ref, rows_ref, acts_ref, key_ref, weight_ref, sem,
):
    loads = []
    for i, (src, dst) in enumerate((
        (picks_hbm, key_ref), (weight_hbm, weight_ref),
        (down_hbm, rows_ref.at[0]), (tok_hbm, acts_ref.at[0]),
        (up_hbm, rows_ref.at[1]), (cot_hbm, acts_ref.at[1]),
    )):
        copy = pltpu.make_async_copy(src, dst, sem.at[i])
        copy.start()
        loads.append(copy)
    coef_ref[...] = jnp.zeros((E, T), f32)
    loads[0].wait()
    first = lax.axis_index("expert") * E
    key = key_ref[...] - first
    own = jnp.logical_and(key >= 0, key < E)
    key_ref[...] = jnp.where(own, key, -1)
    rounds = jnp.max(jnp.sum(own.astype(jnp.int32), axis=0, keepdims=True))
    loads[1].wait()

    def one_round(_, last):
        keys = key_ref[...]
        now = jnp.max(jnp.where(keys < last, keys, -1), axis=0, keepdims=True)
        total = jnp.sum(
            jnp.where(keys == now, weight_ref[...], 0.0), axis=0, keepdims=True
        )
        ids = lax.broadcasted_iota(jnp.int32, (E, T), 0)
        coef_ref[...] = jnp.where(ids == now, total, coef_ref[...])
        return now

    lax.fori_loop(0, rounds, one_round, jnp.full((1, T), E, jnp.int32))
    for copy in loads[2:]:
        copy.wait()


def coefficients(picks, weights, down_rows, tokens, up_rows, out_grad):
    vmem = pl.BlockSpec(memory_space=pltpu.VMEM)
    hbm = pl.BlockSpec(memory_space=pltpu.HBM)
    return pl.pallas_call(
        coefficient_kernel,
        out_shape=(
            pltpu.VMEM((E, T), f32),
            pltpu.VMEM((2, E, D), bf16),
            pltpu.VMEM((2, T, D), bf16),
        ),
        in_specs=[hbm] * 6,
        out_specs=(vmem, vmem, vmem),
        scratch_shapes=[
            pltpu.VMEM((NP, T), jnp.int32),
            pltpu.VMEM((NP, T), f32),
            pltpu.SemaphoreType.DMA((6,)),
        ],
        compiler_params=pltpu.CompilerParams(vmem_limit_bytes=24 * 1024 * 1024),
    )(picks, weights, down_rows, tokens, up_rows, out_grad)


def main_kernel(
    coef, rows, acts, dm_hbm, dv_hbm, um_hbm, uv_hbm,
    layer_ref, input_ref, down_ref, up_ref,
    prow, ws, pws, state,
    gbuf, y1, y2, xbuf, x1, x2, asum, arecv,
    zbuf, z1, z2, z3, z4, bsum, brecv, fin, fpeer,
    load_sem, pair_send, pair_recv, y_send, y_recv, x_send, x_recv,
    z_send, z_recv, a_send, a_recv, b_send, b_recv,
):
    y = lax.axis_index("dp")
    e = lax.axis_index("expert")
    c = lax.rem(e, 2)
    z = lax.rem(e // 2, ZN)
    x = e // (2 * ZN)

    def at(xx, zz):
        return (y, (xx * ZN + zz) * 2 + c)

    def xat(k):
        return lax.rem(x + k + XN, XN)

    def zat(k):
        return lax.rem(z + k + ZN, ZN)

    def yat(k):
        return lax.rem(y + k + YN, YN)

    sibling = (y, (x * ZN + z) * 2 + 1 - c)

    loads = []
    for i, (src, dst) in enumerate((
        (dm_hbm, state.at[0]), (dv_hbm, state.at[1]),
        (um_hbm, state.at[2]), (uv_hbm, state.at[3]),
    )):
        copy = pltpu.make_async_copy(src, dst, load_sem.at[i])
        copy.start()
        loads.append(copy)

    barrier = pltpu.get_barrier_semaphore()
    greet = [sibling, (yat(1), e), (yat(-1), e)]
    greet += [at(xat(k), z) for k in range(1, XN)]
    greet += [at(x, zat(k)) for k in range(1, ZN)]
    for who in greet:
        pl.semaphore_signal(barrier, inc=1, device_id=who, device_id_type=MESH)

    def remote(src, dst, send, recv, who):
        return pltpu.make_async_remote_copy(
            src_ref=src, dst_ref=dst, send_sem=send, recv_sem=recv,
            device_id=who, device_id_type=MESH,
        )

    def y_copy(q, kind, way):
        low = (kind != 1) == (way == 0)
        near = 1 if way == 0 else -1
        block = yat(2 if kind == 0 else near)
        half = pl.ds(0 if low else OWN // 2, OWN // 2)
        src = gbuf.at[q, block, half, :]
        dst = y1.at[way, q] if kind == 0 else y2.at[way, q, half, :]
        sems = y_send.at[kind, way, q], y_recv.at[kind, way, q]
        return remote(src, dst, *sems, (yat(near), e))

    def x_copy(q, kind, way):
        low = (kind != 1) == (way == 0)
        near = 1 if way == 0 else -1
        block = xat(2 if kind == 0 else near)
        half = pl.ds(0 if low else ZN // 2, ZN // 2)
        src = xbuf.at[block, q, half]
        dst = x1.at[way, q] if kind == 0 else x2.at[way, q, half]
        sems = x_send.at[kind, way, q], x_recv.at[kind, way, q]
        return remote(src, dst, *sems, at(xat(near), z))

    def z_copy(q, kind, way):
        low = (kind != 1) == (way == 0)
        near = 1 if way == 0 else -1
        block = zat((4, 3, 3, 2, 1)[kind] * near)
        half = pl.ds(0 if low else XN // 2, XN // 2)
        src = zbuf.at[block, q] if kind > 2 else zbuf.at[block, q, half]
        if kind == 0:
            dst = z1.at[way, q]
        elif kind < 3:
            dst = z2.at[way, q, half]
        else:
            dst = (z3 if kind == 3 else z4).at[way, q]
        sems = z_send.at[kind, way, q], z_recv.at[kind, way, q]
        return remote(src, dst, *sems, at(x, zat(near)))

    def a_copy(q, k):
        p = zat(k + 1)
        sems = a_send.at[q, k], a_recv.at[q, k]
        return remote(asum.at[q, p], arecv.at[q, k], *sems, at(x, p))

    def b_copy(q, k):
        p = xat(k + 1)
        sems = b_send.at[q, k], b_recv.at[q, k]
        return remote(bsum.at[q, p], brecv.at[q, k], *sems, at(p, z))

    s = lax.dot_general(
        rows[0], acts[0], (((1,), (1,)), ((), ())), preferred_element_type=f32
    ) * INV
    b = lax.dot_general(
        rows[1], acts[1], (((1,), (1,)), ((), ())), preferred_element_type=f32
    )
    k = coef[...]
    u = jnp.tanh(gelu_root * (s + gelu_cube * s * s * s))
    ws[1] = (k * (0.5 * s * (1.0 + u))).astype(bf16)
    slope = 0.5 * (1.0 + u) + 0.5 * s * (1.0 - u * u) * gelu_root * (
        1.0 + 3.0 * gelu_cube * s * s
    )
    ws[0] = (k * slope * b).astype(bf16)
    pl.semaphore_wait(barrier, len(greet))
    send_rows = remote(rows.at[c], prow, pair_send.at[0], pair_recv.at[0], sibling)
    send_rows.start()
    send_ws = remote(ws.at[c], pws, pair_send.at[1], pair_recv.at[1], sibling)
    send_ws.start()

    def gradients(q):
        a, first = divmod(q * CW, D)
        g = jnp.dot(ws[a], acts[a, :, first : first + CW], preferred_element_type=f32)
        gbuf[q] = g.astype(bf16).reshape(YN, OWN, CW)
        for kind in (0, 1):
            for way in (0, 1):
                y_copy(q, kind, way).start()

    def partial_rows(block, tokens):
        cols = pl.ds(pl.multiple_of(block * 512, 512), 512)
        part = lax.dot_general(
            rows[1 - c, :, cols], ws[1 - c, :, tokens], (((0,), (0,)), ((), ())),
            preferred_element_type=f32,
        ) + lax.dot_general(
            prow[:, cols], pws[:, tokens], (((0,), (0,)), ((), ())),
            preferred_element_type=f32,
        )
        return part.astype(bf16)

    a_tokens, b_tokens = slice(0, TA), slice(TA, T)

    gradients(0)
    send_rows.wait_recv()
    send_ws.wait_recv()
    for i in range(XN):
        part = partial_rows(i, b_tokens)
        for j in range(ZN):
            for q in range(Q):
                r = j * 64 + q * R
                zbuf[j, q, i] = part[r : r + R, :]
    for q in range(Q):
        for way in (0, 1):
            z_copy(q, 0, way).start()
    for q in range(Q):
        for way in (0, 1):
            z_copy(q, 1, way).start()
    for step in (2, 1, -1, 0):
        block = xat(step)
        part = partial_rows(block, a_tokens)
        for j in range(ZN):
            for q in range(Q):
                r = j * 64 + q * R
                xbuf[block, q, j] = part[r : r + R, :]
        for q in range(Q):
            if step == 2:
                x_copy(q, 0, 0).start()
                x_copy(q, 0, 1).start()
            elif step:
                x_copy(q, 1, 0 if step == 1 else 1).start()
        if step == 2:
            gradients(1)
    gradients(2)
    gradients(3)

    def z_relay(q, kind):
        for way in (0, 1):
            near = 1 if way == 0 else -1
            if kind == 0:
                z_copy(q, 0, way).wait_recv()
                block = zat(3 * near)
                half = pl.ds(0 if way == 0 else XN // 2, XN // 2)
                mine = zbuf[block, q, half].astype(f32)
                zbuf[block, q, half] = (mine + z1[way, q].astype(f32)).astype(bf16)
                z_copy(q, 2, way).start()
            else:
                if kind == 2:
                    z_copy(q, 1, way).wait_recv()
                z_copy(q, kind, way).wait_recv()
                block = zat((2 if kind == 2 else 1) * near)
                got = (z2 if kind == 2 else z3)[way, q].astype(f32)
                zbuf[block, q] = (zbuf[block, q].astype(f32) + got).astype(bf16)
                z_copy(q, kind + 1, way).start()

    def x_relay(q):
        for way in (0, 1):
            x_copy(q, 0, way).wait_recv()
            block = xat(1 if way == 0 else -1)
            half = pl.ds(0 if way == 0 else ZN // 2, ZN // 2)
            mine = xbuf[block, q, half].astype(f32)
            xbuf[block, q, half] = (mine + x1[way, q].astype(f32)).astype(bf16)
            x_copy(q, 2, way).start()

    def y_relay(q):
        for way in (0, 1):
            y_copy(q, 0, way).wait_recv()
            block = yat(1 if way == 0 else -1)
            half = pl.ds(0 if way == 0 else OWN // 2, OWN // 2)
            mine = gbuf[q, block, half, :].astype(f32)
            gbuf[q, block, half, :] = (mine + y1[way, q].astype(f32)).astype(bf16)
            y_copy(q, 2, way).start()

    def x_finish(q):
        for way in (0, 1):
            x_copy(q, 1, way).wait_recv()
            x_copy(q, 2, way).wait_recv()
        total = xbuf[x, q].astype(f32) + x2[0, q].astype(f32) + x2[1, q].astype(f32)
        asum[q] = total.astype(bf16)
        for k in (3, 2, 4, 1, 5, 0, 6):
            a_copy(q, k).start()

    def z_finish(q):
        for way in (0, 1):
            z_copy(q, 4, way).wait_recv()
        total = zbuf[z, q].astype(f32) + z4[0, q].astype(f32) + z4[1, q].astype(f32)
        bsum[q] = total.astype(bf16)
        for k in (1, 0, 2):
            b_copy(q, k).start()

    def adam(q):
        for way in (0, 1):
            y_copy(q, 1, way).wait_recv()
            y_copy(q, 2, way).wait_recv()
        a, first = divmod(q * CW, D)

        def adam_step(i, carry):
            r = pl.ds(pl.multiple_of(i * 16, 16), 16)
            cols = pl.ds(first, CW)
            grad = (
                gbuf[q, y, r, :].astype(f32)
                + y2[0, q, r, :].astype(f32)
                + y2[1, q, r, :].astype(f32)
            )
            if a == 0:
                grad = grad * INV
            m = beta_one * state[2 * a, r, cols] + (1.0 - beta_one) * grad
            v = beta_two * state[2 * a + 1, r, cols] + (1.0 - beta_two) * grad * grad
            old = rows[a, pl.ds(pl.multiple_of(y * OWN + i * 16, 16), 16), cols]
            new = old.astype(f32) - learn_rate * m / (jnp.sqrt(v) + adam_eps)
            (down_ref if a == 0 else up_ref)[r, cols] = new.astype(bf16)
            return carry

        lax.fori_loop(0, OWN // 16, adam_step, 0)

    scale = jnp.where(c == 1, INV, 1.0).astype(f32)

    def finish(q):
        place = q * R // 32, pl.ds(q * R % 32, R)
        total = bsum[q, x].astype(f32)
        for k in range(XN - 1):
            b_copy(q, k).wait_recv()
            total = total + brecv[q, k].astype(f32)
        fin[place[0], place[1], b_tokens] = (total * scale).astype(bf16)
        total = asum[q, z].astype(f32)
        for k in range(ZN - 1):
            a_copy(q, k).wait_recv()
            total = total + arecv[q, k].astype(f32)
        fin[place[0], place[1], a_tokens] = (total * scale).astype(bf16)

    every = range(Q)
    for q in every:
        z_relay(q, 0)
    for q in every:
        x_relay(q)
    y_relay(0)
    for q in every:
        z_relay(q, 2)
    y_relay(1)
    y_relay(2)
    y_relay(3)
    for q in every:
        z_relay(q, 3)
    for q in every:
        x_finish(q)
    for q in every:
        z_finish(q)
    for copy in loads:
        copy.wait()
    adam(0)
    adam(1)
    for q in every:
        finish(q)
    send_fin = remote(fin.at[1 - c], fpeer, pair_send.at[2], pair_recv.at[2], sibling)
    send_fin.start()
    adam(2)
    adam(3)
    mine = fin[c]
    send_fin.wait_recv()
    peer = fpeer[...]
    layer_ref[...] = jnp.where(c == 0, mine, peer)
    input_ref[...] = jnp.where(c == 0, peer, mine)

    send_rows.wait_send()
    send_ws.wait_send()
    send_fin.wait_send()
    for way in (0, 1):
        for q in range(C):
            for kind in range(3):
                y_copy(q, kind, way).wait_send()
        for q in range(Q):
            for kind in range(3):
                x_copy(q, kind, way).wait_send()
            for kind in range(5):
                z_copy(q, kind, way).wait_send()
    for q in range(Q):
        for k in range(ZN - 1):
            a_copy(q, k).wait_send()
        for k in range(XN - 1):
            b_copy(q, k).wait_send()


def exchange(coef, rows, acts, dm, dv, um, uv):
    hbm = pl.BlockSpec(memory_space=pltpu.HBM)
    vmem = pl.BlockSpec(memory_space=pltpu.VMEM)
    dma = pltpu.SemaphoreType.DMA
    return pl.pallas_call(
        main_kernel,
        out_shape=(
            pltpu.VMEM((32, T), bf16),
            pltpu.VMEM((32, T), bf16),
            pltpu.VMEM((OWN, D), bf16),
            pltpu.VMEM((OWN, D), bf16),
        ),
        in_specs=[vmem] * 3 + [hbm] * 4,
        out_specs=(vmem,) * 4,
        scratch_shapes=[
            pltpu.VMEM((E, D), bf16),
            pltpu.VMEM((2, E, T), bf16),
            pltpu.VMEM((E, T), bf16),
            pltpu.VMEM((4, OWN, D), f32),
            pltpu.VMEM((C, YN, OWN, CW), bf16),
            pltpu.VMEM((2, C, OWN // 2, CW), bf16),
            pltpu.VMEM((2, C, OWN, CW), bf16),
            pltpu.VMEM((XN, Q, ZN, R, TA), bf16),
            pltpu.VMEM((2, Q, ZN // 2, R, TA), bf16),
            pltpu.VMEM((2, Q, ZN, R, TA), bf16),
            pltpu.VMEM((Q, ZN, R, TA), bf16),
            pltpu.VMEM((Q, ZN - 1, R, TA), bf16),
            pltpu.VMEM((ZN, Q, XN, R, TB), bf16),
            pltpu.VMEM((2, Q, XN // 2, R, TB), bf16),
            pltpu.VMEM((2, Q, XN, R, TB), bf16),
            pltpu.VMEM((2, Q, XN, R, TB), bf16),
            pltpu.VMEM((2, Q, XN, R, TB), bf16),
            pltpu.VMEM((Q, XN, R, TB), bf16),
            pltpu.VMEM((Q, XN - 1, R, TB), bf16),
            pltpu.VMEM((2, 32, T), bf16),
            pltpu.VMEM((32, T), bf16),
            dma((4,)),
            dma((3,)),
            dma((3,)),
            dma((3, 2, C)),
            dma((3, 2, C)),
            dma((3, 2, Q)),
            dma((3, 2, Q)),
            dma((5, 2, Q)),
            dma((5, 2, Q)),
            dma((Q, ZN - 1)),
            dma((Q, ZN - 1)),
            dma((Q, XN - 1)),
            dma((Q, XN - 1)),
        ],
        compiler_params=pltpu.CompilerParams(
            collective_id=0, has_side_effects=True, vmem_limit_bytes=36 * 1024 * 1024
        ),
    )(coef, rows, acts, dm, dv, um, uv)


def write_kernel(*refs):
    copies = [pltpu.make_async_copy(refs[i], refs[4 + i], refs[8].at[i]) for i in range(4)]
    for copy in copies:
        copy.start()
    for copy in copies:
        copy.wait()


def write_out(*arrays):
    return pl.pallas_call(
        write_kernel,
        out_shape=tuple(jax.ShapeDtypeStruct(a.shape, a.dtype) for a in arrays),
        in_specs=[pl.BlockSpec(memory_space=pltpu.VMEM)] * 4,
        out_specs=(pl.BlockSpec(memory_space=pltpu.HBM),) * 4,
        scratch_shapes=[pltpu.SemaphoreType.DMA((4,))],
        compiler_params=pltpu.CompilerParams(vmem_limit_bytes=4 * 1024 * 1024),
    )(*(pltpu.with_memory_space_constraint(a, pltpu.VMEM) for a in arrays))


def local(
    tokens, picks, route_weight, out_grad, down_rows, up_rows, down_mom, down_var, up_mom, up_var
):
    picks_t = picks.transpose(1, 2, 0).reshape(NP, T)
    weight_t = route_weight.transpose(1, 2, 0).reshape(NP, T)
    in_hbm = functools.partial(pltpu.with_memory_space_constraint, memory_space=pltpu.HBM)
    coef, rows, acts = coefficients(
        *map(in_hbm, (picks_t, weight_t, down_rows, tokens, up_rows, out_grad))
    )
    layer, grad, new_down, new_up = write_out(*exchange(
        coef, rows, acts, *map(in_hbm, (down_mom, down_var, up_mom, up_var))
    ))
    return (layer.T, grad.T, new_down, new_up)


def solution(mesh):
    placed = (
        P("dp", None),
        P("dp", None, None),
        P("dp", None, None),
        P("dp", None),
        P("expert", None),
        P("expert", None),
        P(("expert", "dp"), None),
        P(("expert", "dp"), None),
        P(("expert", "dp"), None),
        P(("expert", "dp"), None),
    )
    return jax.shard_map(
        local,
        mesh=mesh,
        in_specs=placed,
        out_specs=(
            P("dp", "expert"),
            P("dp", "expert"),
            P(("expert", "dp"), None),
            P(("expert", "dp"), None),
        ),
        check_vma=False,
    )
```

time: 51.8 us -> 42.8 us (0.83)
  Pallas kernels: 48.4 us -> 42.1 us
  local copies, waits for them, and re-layouts: 2.64 us -> 0 us
    pallas_call x1 -> x2, Pallas kernels: 45.3 us -> 39 us  [the longest x1 38.1 us: exchange(): pl.pallas_call(main_kernel, out_shape=(pltpu.VMEM((32, T), bf16), pltpu.V...]
    unnamed x4 -> x0, local copies, waits for them, and re-layouts: 2.64 us -> none
where the time goes in v3:
time: 42.8 us; the launch traced here: 42.7 us
  Pallas kernels  42.1 us (98%)
  between operations  0.65 us (2%)
    pallas_call x1, Pallas kernels, exchange(): pl.pallas_call(main_kernel, out_shape=(pltpu.VMEM((32, T), bf16), pltpu.V...  38.1 us
    pallas_call x1, Pallas kernels, coefficients(): pl.pallas_call(coefficient_kernel, out_shape=(pltpu.VMEM((E, T), f32), pl...  3.1 us

profile of v3, /device:TPU:1, one launch (start us, length us, event | category | flops | bytes accessed | tf_op | source)
XLA Modules:
  0.0 42.7 jit_solution(14691706062827187038)
XLA Ops:
  0.6 3.1 %shard_map.129 = (f32[256,512]{1,0:T(8,128)S(1)}, bf16[2,256,2048]{2,1,0:T(8,128)(2,1)S(1)}, bf16[2,512,2048]{2,1,0:T(8,128)(2,1)S(1)}) custom-call(s32[128,512]{1,0:T(8,128)} %bitcast.8, f32[128,512]{1,0:T(8,128)} %bitcast.9, bf16[256,2048]{1,0:T(8,128)(2,1)} %down_hbm.1, bf16[512,2048]{1,0:T(8,128)(2,1)} %tok_hbm.1, bf16[256,2048]{1,0:T(8,128)(2,1)} %up_hbm.1, ...), custom_call_target="tpu_custom_call" | custom-call | tf_op jit(solution)/shard_map/pallas_call | solution.py:76
  3.7 38.1 %shard_map.130 = (bf16[32,512]{1,0:T(8,128)(2,1)S(1)}, bf16[32,512]{1,0:T(8,128)(2,1)S(1)}, bf16[64,2048]{1,0:T(8,128)(2,1)S(1)}, bf16[64,2048]{1,0:T(8,128)(2,1)S(1)}) custom-call(f32[256,512]{1,0:T(8,128)S(1)} %get-tuple-element.15.coef, bf16[2,256,2048]{2,1,0:T(8,128)(2,1)S(1)} %get-tuple-element.16.rows, ...), custom_call_target="tpu_custom_call" | custom-call | tf_op jit(solution)/shard_map/pallas_call | solution.py:413
  41.9 0.8 %shard_map.131 = (bf16[32,512]{1,0:T(8,128)(2,1)}, bf16[32,512]{1,0:T(8,128)(2,1)}, bf16[64,2048]{1,0:T(8,128)(2,1)}, bf16[64,2048]{1,0:T(8,128)(2,1)}) custom-call(bf16[32,512]{1,0:T(8,128)(2,1)S(1)} %get-tuple-element.18.refs_0_, bf16[32,512]{1,0:T(8,128)(2,1)S(1)} %get-tuple-element.19.refs_1_, bf16[64,2048]{1,0:T(8,128)(2,1)S(1)} %get-tuple-element.20.refs_2_, ...), custom_call_target="tpu_custom_call" | custom-call | tf_op jit(solution)/shard_map/pallas_call | solution.py:474

commit v4 on v3

--- a/solution.py
+++ b/solution.py
@@ -95,7 +95,7 @@
     coef, rows, acts, dm_hbm, dv_hbm, um_hbm, uv_hbm,
     layer_ref, input_ref, down_ref, up_ref,
     prow, ws, pws, state,
-    gbuf, y1, y2, xbuf, x1, x2, asum, arecv,
+    gbuf, y1, y2, xbuf, x2, asum, arecv,
     zbuf, z1, z2, z3, z4, bsum, brecv, fin, fpeer,
     load_sem, pair_send, pair_recv, y_send, y_recv, x_send, x_recv,
     z_send, z_recv, a_send, a_recv, b_send, b_recv,
@@ -106,8 +106,8 @@
     z = lax.rem(e // 2, ZN)
     x = e // (2 * ZN)
 
-    def at(xx, zz):
-        return (y, (xx * ZN + zz) * 2 + c)
+    def at(xx, zz, cc=c):
+        return (y, (xx * ZN + zz) * 2 + cc)
 
     def xat(k):
         return lax.rem(x + k + XN, XN)
@@ -131,8 +131,9 @@
 
     barrier = pltpu.get_barrier_semaphore()
     greet = [sibling, (yat(1), e), (yat(-1), e)]
-    greet += [at(xat(k), z) for k in range(1, XN)]
-    greet += [at(x, zat(k)) for k in range(1, ZN)]
+    for cc in (c,):
+        greet += [at(xat(k), z, cc) for k in range(1, XN)]
+        greet += [at(x, zat(k), cc) for k in range(1, ZN)]
     for who in greet:
         pl.semaphore_signal(barrier, inc=1, device_id=who, device_id_type=MESH)
 
@@ -152,15 +153,10 @@
         sems = y_send.at[kind, way, q], y_recv.at[kind, way, q]
         return remote(src, dst, *sems, (yat(near), e))
 
-    def x_copy(q, kind, way):
-        low = (kind != 1) == (way == 0)
-        near = 1 if way == 0 else -1
-        block = xat(2 if kind == 0 else near)
-        half = pl.ds(0 if low else ZN // 2, ZN // 2)
-        src = xbuf.at[block, q, half]
-        dst = x1.at[way, q] if kind == 0 else x2.at[way, q, half]
-        sems = x_send.at[kind, way, q], x_recv.at[kind, way, q]
-        return remote(src, dst, *sems, at(xat(near), z))
+    def x_copy(q, k):
+        p = xat(k + 1)
+        sems = x_send.at[q, k], x_recv.at[q, k]
+        return remote(xbuf.at[p, q], x2.at[k, q], *sems, at(p, z))
 
     def z_copy(q, kind, way):
         low = (kind != 1) == (way == 0)
@@ -187,9 +183,18 @@
         sems = b_send.at[q, k], b_recv.at[q, k]
         return remote(bsum.at[q, p], brecv.at[q, k], *sems, at(p, z))
 
+    def pair_copy(i, src, dst):
+        return remote(src, dst, pair_send.at[i], pair_recv.at[i], sibling)
+
+    send_rows = pair_copy(0, rows.at[c], prow)
+    send_ws = pair_copy(1, ws.at[c], pws)
+    send_fin = pair_copy(2, fin.at[1 - c], fpeer)
+
     s = lax.dot_general(
         rows[0], acts[0], (((1,), (1,)), ((), ())), preferred_element_type=f32
     ) * INV
+    pl.semaphore_wait(barrier, len(greet))
+    send_rows.start()
     b = lax.dot_general(
         rows[1], acts[1], (((1,), (1,)), ((), ())), preferred_element_type=f32
     )
@@ -200,17 +205,13 @@
         1.0 + 3.0 * gelu_cube * s * s
     )
     ws[0] = (k * slope * b).astype(bf16)
-    pl.semaphore_wait(barrier, len(greet))
-    send_rows = remote(rows.at[c], prow, pair_send.at[0], pair_recv.at[0], sibling)
-    send_rows.start()
-    send_ws = remote(ws.at[c], pws, pair_send.at[1], pair_recv.at[1], sibling)
     send_ws.start()
 
     def gradients(q):
         a, first = divmod(q * CW, D)
         g = jnp.dot(ws[a], acts[a, :, first : first + CW], preferred_element_type=f32)
         gbuf[q] = g.astype(bf16).reshape(YN, OWN, CW)
-        for kind in (0, 1):
+        for kind in (0, 1) if q == 0 else (0,):
             for way in (0, 1):
                 y_copy(q, kind, way).start()
 
@@ -239,9 +240,8 @@
     for q in range(Q):
         for way in (0, 1):
             z_copy(q, 0, way).start()
-    for q in range(Q):
-        for way in (0, 1):
-            z_copy(q, 1, way).start()
+    for way in (0, 1):
+        z_copy(0, 1, way).start()
     for step in (2, 1, -1, 0):
         block = xat(step)
         part = partial_rows(block, a_tokens)
@@ -249,16 +249,16 @@
             for q in range(Q):
                 r = j * 64 + q * R
                 xbuf[block, q, j] = part[r : r + R, :]
-        for q in range(Q):
-            if step == 2:
-                x_copy(q, 0, 0).start()
-                x_copy(q, 0, 1).start()
-            elif step:
-                x_copy(q, 1, 0 if step == 1 else 1).start()
-        if step == 2:
+        if step:
+            x_copy(0, step - 1 if step > 0 else 2).start()
+        if step == -1:
+            for k in (1, 0, 2):
+                x_copy(1, k).start()
             gradients(1)
     gradients(2)
     gradients(3)
+    for way in (0, 1):
+        y_copy(1, 1, way).start()
 
     def z_relay(q, kind):
         for way in (0, 1):
@@ -270,6 +270,8 @@
                 mine = zbuf[block, q, half].astype(f32)
                 zbuf[block, q, half] = (mine + z1[way, q].astype(f32)).astype(bf16)
                 z_copy(q, 2, way).start()
+                if q + 1 < Q:
+                    z_copy(q + 1, 1, way).start()
             else:
                 if kind == 2:
                     z_copy(q, 1, way).wait_recv()
@@ -279,15 +281,6 @@
                 zbuf[block, q] = (zbuf[block, q].astype(f32) + got).astype(bf16)
                 z_copy(q, kind + 1, way).start()
 
-    def x_relay(q):
-        for way in (0, 1):
-            x_copy(q, 0, way).wait_recv()
-            block = xat(1 if way == 0 else -1)
-            half = pl.ds(0 if way == 0 else ZN // 2, ZN // 2)
-            mine = xbuf[block, q, half].astype(f32)
-            xbuf[block, q, half] = (mine + x1[way, q].astype(f32)).astype(bf16)
-            x_copy(q, 2, way).start()
-
     def y_relay(q):
         for way in (0, 1):
             y_copy(q, 0, way).wait_recv()
@@ -296,12 +289,14 @@
             mine = gbuf[q, block, half, :].astype(f32)
             gbuf[q, block, half, :] = (mine + y1[way, q].astype(f32)).astype(bf16)
             y_copy(q, 2, way).start()
+            if q + 2 < C:
+                y_copy(q + 2, 1, way).start()
 
     def x_finish(q):
-        for way in (0, 1):
-            x_copy(q, 1, way).wait_recv()
-            x_copy(q, 2, way).wait_recv()
-        total = xbuf[x, q].astype(f32) + x2[0, q].astype(f32) + x2[1, q].astype(f32)
+        total = xbuf[x, q].astype(f32)
+        for k in (2, 0, 1):
+            x_copy(q, k).wait_recv()
+            total = total + x2[k, q].astype(f32)
         asum[q] = total.astype(bf16)
         for k in (3, 2, 4, 1, 5, 0, 6):
             a_copy(q, k).start()
@@ -342,44 +337,39 @@
     scale = jnp.where(c == 1, INV, 1.0).astype(f32)
 
     def finish(q):
-        place = q * R // 32, pl.ds(q * R % 32, R)
+        total = asum[q, z].astype(f32)
+        for k in range(ZN - 1):
+            a_copy(q, k).wait_recv()
+            total = total + arecv[q, k].astype(f32)
+        fin[q, :, a_tokens] = (total * scale).astype(bf16)
         total = bsum[q, x].astype(f32)
         for k in range(XN - 1):
             b_copy(q, k).wait_recv()
             total = total + brecv[q, k].astype(f32)
-        fin[place[0], place[1], b_tokens] = (total * scale).astype(bf16)
-        total = asum[q, z].astype(f32)
-        for k in range(ZN - 1):
-            a_copy(q, k).wait_recv()
-            total = total + arecv[q, k].astype(f32)
-        fin[place[0], place[1], a_tokens] = (total * scale).astype(bf16)
-
-    every = range(Q)
-    for q in every:
-        z_relay(q, 0)
-    for q in every:
-        x_relay(q)
+        fin[q, :, b_tokens] = (total * scale).astype(bf16)
+
+    z_relay(0, 0)
+    z_relay(1, 0)
+    z_relay(0, 2)
+    z_relay(1, 2)
     y_relay(0)
-    for q in every:
-        z_relay(q, 2)
     y_relay(1)
+    z_relay(0, 3)
+    z_relay(1, 3)
+    x_finish(0)
     y_relay(2)
     y_relay(3)
-    for q in every:
-        z_relay(q, 3)
-    for q in every:
-        x_finish(q)
-    for q in every:
-        z_finish(q)
+    x_finish(1)
+    z_finish(0)
+    z_finish(1)
     for copy in loads:
         copy.wait()
     adam(0)
     adam(1)
-    for q in every:
-        finish(q)
-    send_fin = remote(fin.at[1 - c], fpeer, pair_send.at[2], pair_recv.at[2], sibling)
+    adam(2)
+    finish(0)
+    finish(1)
     send_fin.start()
-    adam(2)
     adam(3)
     mine = fin[c]
     send_fin.wait_recv()
@@ -395,14 +385,13 @@
             for kind in range(3):
                 y_copy(q, kind, way).wait_send()
         for q in range(Q):
-            for kind in range(3):
-                x_copy(q, kind, way).wait_send()
             for kind in range(5):
                 z_copy(q, kind, way).wait_send()
     for q in range(Q):
         for k in range(ZN - 1):
             a_copy(q, k).wait_send()
         for k in range(XN - 1):
+            x_copy(q, k).wait_send()
             b_copy(q, k).wait_send()
 
 
@@ -429,26 +418,25 @@
             pltpu.VMEM((2, C, OWN // 2, CW), bf16),
             pltpu.VMEM((2, C, OWN, CW), bf16),
             pltpu.VMEM((XN, Q, ZN, R, TA), bf16),
-            pltpu.VMEM((2, Q, ZN // 2, R, TA), bf16),
-            pltpu.VMEM((2, Q, ZN, R, TA), bf16),
+            pltpu.VMEM((XN - 1, Q, ZN, R, TA), bf16),
             pltpu.VMEM((Q, ZN, R, TA), bf16),
-            pltpu.VMEM((Q, ZN - 1, R, TA), bf16),
+            pltpu.VMEM((2, ZN - 1, R, TA), bf16),
             pltpu.VMEM((ZN, Q, XN, R, TB), bf16),
             pltpu.VMEM((2, Q, XN // 2, R, TB), bf16),
             pltpu.VMEM((2, Q, XN, R, TB), bf16),
             pltpu.VMEM((2, Q, XN, R, TB), bf16),
             pltpu.VMEM((2, Q, XN, R, TB), bf16),
             pltpu.VMEM((Q, XN, R, TB), bf16),
-            pltpu.VMEM((Q, XN - 1, R, TB), bf16),
+            pltpu.VMEM((2, XN - 1, R, TB), bf16),
             pltpu.VMEM((2, 32, T), bf16),
             pltpu.VMEM((32, T), bf16),
             dma((4,)),
-            dma((3,)),
-            dma((3,)),
+            dma((4,)),
+            dma((4,)),
             dma((3, 2, C)),
             dma((3, 2, C)),
-            dma((3, 2, Q)),
-            dma((3, 2, Q)),
+            dma((Q, XN - 1)),
+            dma((Q, XN - 1)),
             dma((5, 2, Q)),
             dma((5, 2, Q)),
             dma((Q, ZN - 1)),

time: 42.8 us -> 40.5 us (0.946)
  Pallas kernels: 42.1 us -> 39.8 us
    pallas_call x1, Pallas kernels: 38.1 us -> 35.9 us  [exchange(): pl.pallas_call(main_kernel, out_shape=(pltpu.VMEM((32, T), bf16), pltpu.V...]
where the time goes in v4:
time: 40.5 us; the launch traced here: 40.4 us
  Pallas kernels  39.8 us (98%)
  between operations  0.65 us (2%)
    pallas_call x1, Pallas kernels, exchange(): pl.pallas_call(main_kernel, out_shape=(pltpu.VMEM((32, T), bf16), pltpu.V...  35.9 us
    pallas_call x1, Pallas kernels, coefficients(): pl.pallas_call(coefficient_kernel, out_shape=(pltpu.VMEM((E, T), f32), pl...  3.1 us
    pallas_call x1, Pallas kernels, write_out(): pl.pallas_call(write_kernel, out_shape=tuple((jax.ShapeDtypeStruct(a.shap...  0.85 us

profile of v4, /device:TPU:1, one launch (start us, length us, event | category | flops | bytes accessed | tf_op | source)
XLA Modules:
  0.0 40.4 jit_solution(10551923003286439619)
XLA Ops:
  0.6 3.1 %shard_map.129 = (f32[256,512]{1,0:T(8,128)S(1)}, bf16[2,256,2048]{2,1,0:T(8,128)(2,1)S(1)}, bf16[2,512,2048]{2,1,0:T(8,128)(2,1)S(1)}) custom-call(s32[128,512]{1,0:T(8,128)} %bitcast.8, f32[128,512]{1,0:T(8,128)} %bitcast.9, bf16[256,2048]{1,0:T(8,128)(2,1)} %down_hbm.1, bf16[512,2048]{1,0:T(8,128)(2,1)} %tok_hbm.1, bf16[256,2048]{1,0:T(8,128)(2,1)} %up_hbm.1, ...), custom_call_target="tpu_custom_call" | custom-call | tf_op jit(solution)/shard_map/pallas_call | solution.py:76
  3.7 35.9 %shard_map.130 = (bf16[32,512]{1,0:T(8,128)(2,1)S(1)}, bf16[32,512]{1,0:T(8,128)(2,1)S(1)}, bf16[64,2048]{1,0:T(8,128)(2,1)S(1)}, bf16[64,2048]{1,0:T(8,128)(2,1)S(1)}) custom-call(f32[256,512]{1,0:T(8,128)S(1)} %get-tuple-element.15.coef, bf16[2,256,2048]{2,1,0:T(8,128)(2,1)S(1)} %get-tuple-element.16.rows, ...), custom_call_target="tpu_custom_call" | custom-call | tf_op jit(solution)/shard_map/pallas_call | solution.py:402
  39.6 0.8 %shard_map.131 = (bf16[32,512]{1,0:T(8,128)(2,1)}, bf16[32,512]{1,0:T(8,128)(2,1)}, bf16[64,2048]{1,0:T(8,128)(2,1)}, bf16[64,2048]{1,0:T(8,128)(2,1)}) custom-call(bf16[32,512]{1,0:T(8,128)(2,1)S(1)} %get-tuple-element.18.refs_0_, bf16[32,512]{1,0:T(8,128)(2,1)S(1)} %get-tuple-element.19.refs_1_, bf16[64,2048]{1,0:T(8,128)(2,1)S(1)} %get-tuple-element.20.refs_2_, ...), custom_call_target="tpu_custom_call" | custom-call | tf_op jit(solution)/shard_map/pallas_call | solution.py:462

commit v5 on v4

--- a/solution.py
+++ b/solution.py
@@ -34,14 +34,14 @@
 
 
 def coefficient_kernel(
-    picks_hbm, weight_hbm, down_hbm, tok_hbm, up_hbm, cot_hbm,
+    picks_hbm, weight_hbm, down_hbm, tok_hbm, up_hbm,
     coef_ref, rows_ref, acts_ref, key_ref, weight_ref, sem,
 ):
     loads = []
     for i, (src, dst) in enumerate((
         (picks_hbm, key_ref), (weight_hbm, weight_ref),
-        (down_hbm, rows_ref.at[0]), (tok_hbm, acts_ref.at[0]),
-        (up_hbm, rows_ref.at[1]), (cot_hbm, acts_ref.at[1]),
+        (down_hbm, rows_ref.at[0]), (tok_hbm, acts_ref),
+        (up_hbm, rows_ref.at[1]),
     )):
         copy = pltpu.make_async_copy(src, dst, sem.at[i])
         copy.start()
@@ -70,7 +70,7 @@
         copy.wait()
 
 
-def coefficients(picks, weights, down_rows, tokens, up_rows, out_grad):
+def coefficients(picks, weights, down_rows, tokens, up_rows):
     vmem = pl.BlockSpec(memory_space=pltpu.VMEM)
     hbm = pl.BlockSpec(memory_space=pltpu.HBM)
     return pl.pallas_call(
@@ -78,23 +78,23 @@
         out_shape=(
             pltpu.VMEM((E, T), f32),
             pltpu.VMEM((2, E, D), bf16),
-            pltpu.VMEM((2, T, D), bf16),
+            pltpu.VMEM((T, D), bf16),
         ),
-        in_specs=[hbm] * 6,
+        in_specs=[hbm] * 5,
         out_specs=(vmem, vmem, vmem),
         scratch_shapes=[
             pltpu.VMEM((NP, T), jnp.int32),
             pltpu.VMEM((NP, T), f32),
-            pltpu.SemaphoreType.DMA((6,)),
+            pltpu.SemaphoreType.DMA((5,)),
         ],
         compiler_params=pltpu.CompilerParams(vmem_limit_bytes=24 * 1024 * 1024),
-    )(picks, weights, down_rows, tokens, up_rows, out_grad)
+    )(picks, weights, down_rows, tokens, up_rows)
 
 
 def main_kernel(
-    coef, rows, acts, dm_hbm, dv_hbm, um_hbm, uv_hbm,
+    coef, rows, tok, cot_hbm, dm_hbm, dv_hbm, um_hbm, uv_hbm,
     layer_ref, input_ref, down_ref, up_ref,
-    prow, ws, pws, state,
+    cot, prow, ws, pws, state,
     gbuf, y1, y2, xbuf, x2, asum, arecv,
     zbuf, z1, z2, z3, z4, bsum, brecv, fin, fpeer,
     load_sem, pair_send, pair_recv, y_send, y_recv, x_send, x_recv,
@@ -122,7 +122,7 @@
 
     loads = []
     for i, (src, dst) in enumerate((
-        (dm_hbm, state.at[0]), (dv_hbm, state.at[1]),
+        (cot_hbm, cot), (dm_hbm, state.at[0]), (dv_hbm, state.at[1]),
         (um_hbm, state.at[2]), (uv_hbm, state.at[3]),
     )):
         copy = pltpu.make_async_copy(src, dst, load_sem.at[i])
@@ -191,12 +191,13 @@
     send_fin = pair_copy(2, fin.at[1 - c], fpeer)
 
     s = lax.dot_general(
-        rows[0], acts[0], (((1,), (1,)), ((), ())), preferred_element_type=f32
+        rows[0], tok[...], (((1,), (1,)), ((), ())), preferred_element_type=f32
     ) * INV
     pl.semaphore_wait(barrier, len(greet))
     send_rows.start()
+    loads[0].wait()
     b = lax.dot_general(
-        rows[1], acts[1], (((1,), (1,)), ((), ())), preferred_element_type=f32
+        rows[1], cot[...], (((1,), (1,)), ((), ())), preferred_element_type=f32
     )
     k = coef[...]
     u = jnp.tanh(gelu_root * (s + gelu_cube * s * s * s))
@@ -209,7 +210,9 @@
 
     def gradients(q):
         a, first = divmod(q * CW, D)
-        g = jnp.dot(ws[a], acts[a, :, first : first + CW], preferred_element_type=f32)
+        g = jnp.dot(
+            ws[a], (tok, cot)[a][:, first : first + CW], preferred_element_type=f32
+        )
         gbuf[q] = g.astype(bf16).reshape(YN, OWN, CW)
         for kind in (0, 1) if q == 0 else (0,):
             for way in (0, 1):
@@ -362,7 +365,7 @@
     x_finish(1)
     z_finish(0)
     z_finish(1)
-    for copy in loads:
+    for copy in loads[1:]:
         copy.wait()
     adam(0)
     adam(1)
@@ -395,7 +398,7 @@
             b_copy(q, k).wait_send()
 
 
-def exchange(coef, rows, acts, dm, dv, um, uv):
+def exchange(coef, rows, tokens, out_grad, dm, dv, um, uv):
     hbm = pl.BlockSpec(memory_space=pltpu.HBM)
     vmem = pl.BlockSpec(memory_space=pltpu.VMEM)
     dma = pltpu.SemaphoreType.DMA
@@ -407,9 +410,10 @@
             pltpu.VMEM((OWN, D), bf16),
             pltpu.VMEM((OWN, D), bf16),
         ),
-        in_specs=[vmem] * 3 + [hbm] * 4,
+        in_specs=[vmem] * 3 + [hbm] * 5,
         out_specs=(vmem,) * 4,
         scratch_shapes=[
+            pltpu.VMEM((T, D), bf16),
             pltpu.VMEM((E, D), bf16),
             pltpu.VMEM((2, E, T), bf16),
             pltpu.VMEM((E, T), bf16),
@@ -430,7 +434,7 @@
             pltpu.VMEM((2, XN - 1, R, TB), bf16),
             pltpu.VMEM((2, 32, T), bf16),
             pltpu.VMEM((32, T), bf16),
-            dma((4,)),
+            dma((5,)),
             dma((4,)),
             dma((4,)),
             dma((3, 2, C)),
@@ -447,7 +451,7 @@
         compiler_params=pltpu.CompilerParams(
             collective_id=0, has_side_effects=True, vmem_limit_bytes=36 * 1024 * 1024
         ),
-    )(coef, rows, acts, dm, dv, um, uv)
+    )(coef, rows, tokens, out_grad, dm, dv, um, uv)
 
 
 def write_kernel(*refs):
@@ -475,11 +479,11 @@
     picks_t = picks.transpose(1, 2, 0).reshape(NP, T)
     weight_t = route_weight.transpose(1, 2, 0).reshape(NP, T)
     in_hbm = functools.partial(pltpu.with_memory_space_constraint, memory_space=pltpu.HBM)
-    coef, rows, acts = coefficients(
-        *map(in_hbm, (picks_t, weight_t, down_rows, tokens, up_rows, out_grad))
+    coef, rows, tokens = coefficients(
+        *map(in_hbm, (picks_t, weight_t, down_rows, tokens, up_rows))
     )
     layer, grad, new_down, new_up = write_out(*exchange(
-        coef, rows, acts, *map(in_hbm, (down_mom, down_var, up_mom, up_var))
+        coef, rows, tokens, *map(in_hbm, (out_grad, down_mom, down_var, up_mom, up_var))
     ))
     return (layer.T, grad.T, new_down, new_up)
 

time: 40.5 us -> 39.8 us (0.983)
  Pallas kernels: 39.8 us -> 39.1 us
    pallas_call x1, Pallas kernels: 3.1 us -> 2.38 us  [coefficients(): pl.pallas_call(coefficient_kernel, out_shape=(pltpu.VMEM((E, T), f32), pl...]
where the time goes in v5:
time: 39.8 us; the launch traced here: 39.7 us
  Pallas kernels  39.1 us (98%)
  between operations  0.65 us (2%)
    pallas_call x1, Pallas kernels, exchange(): pl.pallas_call(main_kernel, out_shape=(pltpu.VMEM((32, T), bf16), pltpu.V...  35.8 us
    pallas_call x1, Pallas kernels, coefficients(): pl.pallas_call(coefficient_kernel, out_shape=(pltpu.VMEM((E, T), f32), pl...  2.38 us
    pallas_call x1, Pallas kernels, write_out(): pl.pallas_call(write_kernel, out_shape=tuple((jax.ShapeDtypeStruct(a.shap...  0.85 us

profile of v5, /device:TPU:1, one launch (start us, length us, event | category | flops | bytes accessed | tf_op | source)
XLA Modules:
  0.0 39.7 jit_solution(16790069019743088474)
XLA Ops:
  0.6 2.4 %shard_map.129 = (f32[256,512]{1,0:T(8,128)S(1)}, bf16[2,256,2048]{2,1,0:T(8,128)(2,1)S(1)}, bf16[512,2048]{1,0:T(8,128)(2,1)S(1)}) custom-call(s32[128,512]{1,0:T(8,128)} %bitcast.8, f32[128,512]{1,0:T(8,128)} %bitcast.9, bf16[256,2048]{1,0:T(8,128)(2,1)} %down_hbm.1, bf16[512,2048]{1,0:T(8,128)(2,1)} %tok_hbm.1, bf16[256,2048]{1,0:T(8,128)(2,1)} %up_hbm.1), custom_call_target="tpu_custom_call" | custom-call | tf_op jit(solution)/shard_map/pallas_call | solution.py:76
  3.0 35.8 %shard_map.130 = (bf16[32,512]{1,0:T(8,128)(2,1)S(1)}, bf16[32,512]{1,0:T(8,128)(2,1)S(1)}, bf16[64,2048]{1,0:T(8,128)(2,1)S(1)}, bf16[64,2048]{1,0:T(8,128)(2,1)S(1)}) custom-call(f32[256,512]{1,0:T(8,128)S(1)} %get-tuple-element.15.coef, bf16[2,256,2048]{2,1,0:T(8,128)(2,1)S(1)} %get-tuple-element.16.rows, bf16[512,2048]{1,0:T(8,128)(2,1)S(1)} %get-tuple-element.17.tok, ...), custom_call_target="tpu_custom_call" | custom-call | tf_op jit(solution)/shard_map/pallas_call | solution.py:405
  38.9 0.8 %shard_map.131 = (bf16[32,512]{1,0:T(8,128)(2,1)}, bf16[32,512]{1,0:T(8,128)(2,1)}, bf16[64,2048]{1,0:T(8,128)(2,1)}, bf16[64,2048]{1,0:T(8,128)(2,1)}) custom-call(bf16[32,512]{1,0:T(8,128)(2,1)S(1)} %get-tuple-element.18.refs_0_, bf16[32,512]{1,0:T(8,128)(2,1)S(1)} %get-tuple-element.19.refs_1_, bf16[64,2048]{1,0:T(8,128)(2,1)S(1)} %get-tuple-element.20.refs_2_, ...), custom_call_target="tpu_custom_call" | custom-call | tf_op jit(solution)/shard_map/pallas_call | solution.py:466

commit v6 on v5

--- a/solution.py
+++ b/solution.py
@@ -369,10 +369,10 @@
         copy.wait()
     adam(0)
     adam(1)
+    finish(1 - c)
+    send_fin.start()
+    finish(c)
     adam(2)
-    finish(0)
-    finish(1)
-    send_fin.start()
     adam(3)
     mine = fin[c]
     send_fin.wait_recv()

time: 39.8 us -> 39.8 us (level)
  no operation moved by 1% of the time
where the time goes in v6:
time: 39.8 us; the launch traced here: 39.7 us
  Pallas kernels  39.1 us (98%)
  between operations  0.65 us (2%)
    pallas_call x1, Pallas kernels, exchange(): pl.pallas_call(main_kernel, out_shape=(pltpu.VMEM((32, T), bf16), pltpu.V...  35.9 us
    pallas_call x1, Pallas kernels, coefficients(): pl.pallas_call(coefficient_kernel, out_shape=(pltpu.VMEM((E, T), f32), pl...  2.38 us
    pallas_call x1, Pallas kernels, write_out(): pl.pallas_call(write_kernel, out_shape=tuple((jax.ShapeDtypeStruct(a.shap...  0.85 us

profile of v6, /device:TPU:1, one launch (start us, length us, event | category | flops | bytes accessed | tf_op | source)
XLA Modules:
  0.0 39.7 jit_solution(1314806855949768389)
XLA Ops:
  0.6 2.4 %shard_map.129 = (f32[256,512]{1,0:T(8,128)S(1)}, bf16[2,256,2048]{2,1,0:T(8,128)(2,1)S(1)}, bf16[512,2048]{1,0:T(8,128)(2,1)S(1)}) custom-call(s32[128,512]{1,0:T(8,128)} %bitcast.8, f32[128,512]{1,0:T(8,128)} %bitcast.9, bf16[256,2048]{1,0:T(8,128)(2,1)} %down_hbm.1, bf16[512,2048]{1,0:T(8,128)(2,1)} %tok_hbm.1, bf16[256,2048]{1,0:T(8,128)(2,1)} %up_hbm.1), custom_call_target="tpu_custom_call" | custom-call | tf_op jit(solution)/shard_map/pallas_call | solution.py:76
  3.0 35.9 %shard_map.130 = (bf16[32,512]{1,0:T(8,128)(2,1)S(1)}, bf16[32,512]{1,0:T(8,128)(2,1)S(1)}, bf16[64,2048]{1,0:T(8,128)(2,1)S(1)}, bf16[64,2048]{1,0:T(8,128)(2,1)S(1)}) custom-call(f32[256,512]{1,0:T(8,128)S(1)} %get-tuple-element.15.coef, bf16[2,256,2048]{2,1,0:T(8,128)(2,1)S(1)} %get-tuple-element.16.rows, bf16[512,2048]{1,0:T(8,128)(2,1)S(1)} %get-tuple-element.17.tok, ...), custom_call_target="tpu_custom_call" | custom-call | tf_op jit(solution)/shard_map/pallas_call | solution.py:405
  38.9 0.8 %shard_map.131 = (bf16[32,512]{1,0:T(8,128)(2,1)}, bf16[32,512]{1,0:T(8,128)(2,1)}, bf16[64,2048]{1,0:T(8,128)(2,1)}, bf16[64,2048]{1,0:T(8,128)(2,1)}) custom-call(bf16[32,512]{1,0:T(8,128)(2,1)S(1)} %get-tuple-element.18.refs_0_, bf16[32,512]{1,0:T(8,128)(2,1)S(1)} %get-tuple-element.19.refs_1_, bf16[64,2048]{1,0:T(8,128)(2,1)S(1)} %get-tuple-element.20.refs_2_, ...), custom_call_target="tpu_custom_call" | custom-call | tf_op jit(solution)/shard_map/pallas_call | solution.py:466
